TPU v7x, 256 devices: a whole 4x4x8 slice. The times are simulated.
256 devices in a mesh: row: 32 (over z, x), col: 2 (over core), depth: 4 (over y).
Axes of the slice: x: 4, y: 4, z: 8, core: 2. Of those that a mesh axis runs over, the one named last changes fastest.
Arguments:
- attn_out: bfloat16 [32768, 3072], P(('depth', 'row'), 'col'), may hold values from -24 to 24
- w_out: bfloat16 [3072, 3072], P('row', 'col'), may hold values from -0.21875 to 0.21875
- cotangent: bfloat16 [32768, 3072], P(('depth', 'row'), 'col'), may hold values from -6 to 6
Outputs:
- projected: bfloat16 [32768, 3072], P(('depth', 'row'), 'col')
- input_grad: bfloat16 [32768, 3072], P(('depth', 'row'), 'col')
- weight_grad: float32 [3072, 3072], P('row', 'col')
All inputs are finite; a program needn't handle non-finite values.
Results may differ from a plain program's by a relative error of at most 0.001.
Values may be sent and summed in bfloat16 or wider, within the bound.
A program may use at most 128 MiB of HBM per device.

v0:
```python
import math

import jax
import jax.numpy as jnp
from jax import lax
from jax.sharding import PartitionSpec as P


def body(attn_out, w_out, cotangent):
    tok_rows = attn_out.shape[0]
    features = lax.all_gather(attn_out, "col", axis=1, tiled=True)
    columns = features
    forward = jnp.dot(
        columns,
        lax.all_gather(w_out, "row", axis=0, tiled=True),
        preferred_element_type=jnp.float32,
    )
    panel = lax.all_gather(w_out, "row", axis=0, tiled=True)
    projected = forward.astype(jnp.bfloat16)
    transposed = lax.psum_scatter(
        lax.dot_general(
            panel, cotangent, (((1,), (1,)), ((), ())), preferred_element_type=jnp.float32
        ),
        "col",
        scatter_dimension=0,
        tiled=True,
    )
    input_grad = transposed.T.astype(jnp.bfloat16)
    columns = features
    row_summed = lax.psum_scatter(
        lax.dot_general(
            columns, cotangent, (((0,), (0,)), ((), ())), preferred_element_type=jnp.float32
        ),
        "row",
        scatter_dimension=0,
        tiled=True,
    )
    total = lax.psum(row_summed, "depth")
    token_total = tok_rows * lax.axis_size("row") * lax.axis_size("depth")
    weight_grad = total * (1.0 / math.sqrt(token_total))
    return (projected, input_grad, weight_grad)


def solution(mesh):
    in_specs = (P(("depth", "row"), "col"), P("row", "col"), P(("depth", "row"), "col"))
    out_specs = (P(("depth", "row"), "col"), P(("depth", "row"), "col"), P("row", "col"))
    return jax.shard_map(body, mesh=mesh, in_specs=in_specs, out_specs=out_specs, check_vma=False)
```

profile of v0, /device:TPU:16, one launch (start us, length us, event | category | flops | bytes accessed | tf_op | source)
XLA Modules:
  0.0 463.5 jit_solution(4483140692312789410)
XLA Ops:
  7.2 0.0 copy-start
  7.2 0.0 all-gather.3.cloned.1.call-start
  7.2 0.7 all-gather.3.cloned.1.call-update
  7.9 0.0 all-gather.5.cloned.1.call-start
  8.0 0.7 all-gather.5.cloned.1.call-update
  8.7 0.0 reduce-scatter.5.cloned.1.call-start
  8.7 19.1 %all-gather.3.cloned.1.call-done = bf16[256,3072]{1,0:T(8,128)(2,1)} async-done(((bf16[256,1536]{1,0:T(8,128)(2,1)}), bf16[256,3072]{1,0:T(8,128)(2,1)}) %all-gather.3.cloned.1.call-update) | async-done | bytes 1572880 | tf_op jit(solution)/shard_map/all_gather | solution.py:11
  27.8 0.0 copy-done
  27.8 9.4 %fusion.1 = f32[3072,1536]{1,0:T(8,128)} fusion(bf16[256,3072]{1,0:T(8,128)(2,1)} %all-gather.3.cloned.1.call-done, bf16[256,1536]{1,0:T(8,128)(2,1)S(1)} %copy-done), kind=kOutput, calls=%fused_computation.4 | convolution fusion | flops 2415919104 | bytes 21233664 | tf_op jit(solution)/shard_map/dot_general | solution.py:31
  37.2 0.0 reduce-scatter.5.cloned.1.call-update
  37.2 0.0 reduce-scatter.3.cloned.1.call-start
  37.3 97.9 %all-gather.5.cloned.1.call-done = bf16[3072,1536]{1,0:T(8,128)(2,1)} async-done(((bf16[96,1536]{1,0:T(8,128)(2,1)}), bf16[3072,1536]{1,0:T(8,128)(2,1)}) %all-gather.5.cloned.1.call-update) | async-done | bytes 9437200 | tf_op jit(solution)/shard_map/all_gather | solution.py:15
  135.2 8.1 %fusion = f32[3072,256]{1,0:T(8,128)} fusion(bf16[3072,1536]{1,0:T(8,128)(2,1)} %all-gather.5.cloned.1.call-done, bf16[256,1536]{1,0:T(8,128)(2,1)S(1)} %copy-done), kind=kOutput, calls=%fused_computation.3 | convolution fusion | flops 2415919104 | bytes 13369344 | tf_op jit(solution)/shard_map/dot_general | solution.py:21
  143.3 0.0 copy-start.1
  143.3 0.0 reduce-scatter.3.cloned.1.call-update
  143.3 0.0 all-reduce.2.cloned.1.call-start
  143.3 243.2 %reduce-scatter.5.cloned.1.call-done = f32[96,1536]{1,0:T(8,128)} async-done(((f32[3072,1536]{1,0:T(8,128)}), f32[96,1536]{1,0:T(8,128)}) %reduce-scatter.5.cloned.1.call-update) | async-done | bytes 589840 | tf_op jit(solution)/shard_map/reduce_scatter | solution.py:30
  386.5 0.0 all-reduce.2.cloned.1.call-update
  386.5 0.0 copy-done.1
  386.5 7.2 %convolution_convert_fusion = bf16[256,1536]{1,0:T(8,128)(2,1)} fusion(bf16[256,3072]{1,0:T(8,128)(2,1)S(1)} %copy-done.1, bf16[3072,1536]{1,0:T(8,128)(2,1)} %all-gather.5.cloned.1.call-done), kind=kOutput, calls=%fused_computation | convolution fusion | flops 2416312320 | bytes 11796480 | tf_op jit(solution)/shard_map/dot_general | solution.py:13
  393.7 9.8 %reduce-scatter.3.cloned.1.call-done = f32[1536,256]{1,0:T(8,128)} async-done(((f32[3072,256]{1,0:T(8,128)}), f32[1536,256]{1,0:T(8,128)}) %reduce-scatter.3.cloned.1.call-update) | async-done | bytes 1572880 | tf_op jit(solution)/shard_map/reduce_scatter | solution.py:20
  403.5 1.5 convert_bitcast_fusion
  405.0 1.2 copy.6
  406.2 48.9 %all-reduce.2.cloned.1.call-done = f32[96,1536]{1,0:T(8,128)} async-done(((f32[96,1536]{1,0:T(8,128)}), f32[96,1536]{1,0:T(8,128)}) %all-reduce.2.cloned.1.call-update) | async-done | bytes 589840 | tf_op jit(solution)/shard_map/psum | solution.py:38
  455.1 1.9 broadcast_multiply_fusion
Async XLA Ops:
  7.2 20.6 %copy-start = (bf16[256,1536]{1,0:T(8,128)(2,1)S(1)}, bf16[256,1536]{1,0:T(8,128)(2,1)}, u32[]{:S(2)}) copy-start(bf16[256,1536]{1,0:T(8,128)(2,1)} %param.5) | copy-start | bytes 2359300
  7.2 20.6 %all-gather.3.cloned.1.call-start = ((), (), s32[]{:S(2)}) async-start(), calls=%async_computation.2 | async-start | bytes 2359296 | tf_op jit(solution)/shard_map/all_gather | solution.py:11
  7.9 127.2 %all-gather.5.cloned.1.call-start = ((), (), s32[]{:S(2)}) async-start(), calls=%async_computation.3 | async-start | bytes 9732096 | tf_op jit(solution)/shard_map/all_gather | solution.py:15
  8.7 377.8 %reduce-scatter.5.cloned.1.call-start = ((), (), s32[]{:S(2)}) async-start(), calls=%async_computation.5 | async-start | bytes 19464192 | tf_op jit(solution)/shard_map/reduce_scatter | solution.py:30
  37.2 366.3 %reduce-scatter.3.cloned.1.call-start = ((), (), s32[]{:S(2)}) async-start(), calls=%async_computation.4 | async-start | bytes 4718592 | tf_op jit(solution)/shard_map/reduce_scatter | solution.py:20
  143.3 243.3 %copy-start.1 = (bf16[256,3072]{1,0:T(8,128)(2,1)S(1)}, bf16[256,3072]{1,0:T(8,128)(2,1)}, u32[]{:S(2)}) copy-start(bf16[256,3072]{1,0:T(8,128)(2,1)} %all-gather.3.cloned.1.call-done) | copy-start | bytes 4718596
  143.3 311.8 %all-reduce.2.cloned.1.call-start = ((), (), s32[]{:S(2)}) async-start(), calls=%async_computation.6 | async-start | bytes 1179648 | tf_op jit(solution)/shard_map/psum | solution.py:38
Sparse Core Ops, SparseCore 0:
  9.8 17.9 all-gather.2
  30.3 104.7 all-gather.4
  139.4 247.0 reduce-scatter.4
  388.9 14.6 reduce-scatter.2
  405.8 49.2 all-reduce.1
where the time goes:
time: 465 us; the launch traced here: 464 us
  waiting for transfers between devices  420 us (90%)
  matrix products  24.7 us (5%)
  between operations  13.8 us (3%)
    reduce_scatter x1, waiting for transfers between devices, body(): lax.psum_scatter(lax.dot_general(columns, cotangent, (((0,), (0,)), ((),...  243 us
    all_gather x1, waiting for transfers between devices, body(): lax.all_gather(w_out, 'row', axis=0, tiled=True)  97.9 us
    psum x1, waiting for transfers between devices, body(): total = lax.psum(row_summed, 'depth')  48.9 us
    all_gather x1, waiting for transfers between devices, body(): features = lax.all_gather(attn_out, 'col', axis=1, tiled=True)  19.1 us
    reduce_scatter x1, waiting for transfers between devices, body(): lax.psum_scatter(lax.dot_general(panel, cotangent, (((1,), (1,)), ((), ()...  9.76 us
    dot_general x1, matrix products, body(): lax.dot_general(columns, cotangent, (((0,), (0,)), ((), ())), preferred_e...  9.44 us
  transfers between devices with their start and end apart: 5, of which 5 were waited for; matrix products, arithmetic and copies ran while one was open for 6% of the time, Pallas kernels for 0%

commit v1 on v0

v1 whole, which is shorter than its diff:
```python
import math

import jax
import jax.numpy as jnp
from jax import lax
from jax.experimental import pallas as pl
from jax.experimental.pallas import tpu as pltpu
from jax.sharding import PartitionSpec as P

MESH = pl.DeviceIdType.MESH
NZ, NX, NY = 8, 4, 4
TOK, HALF, BLK = 256, 1536, 96
MAIN, TILE = 1024, 128
WIDE = MAIN + TILE
QUART = HALF // NY
R1 = 64
S1 = 48
F32, BF16 = jnp.float32, jnp.bfloat16
N_MSG = 200


def kernel(attn, w, cot, proj, igrad, wgrad, A, CQ, Wp, Wr, cotp, G, bo, bm, br,
           xa, xb, za, zb, za4, ya, yb, yxa, yxb, send, recv):
    row, c, y = lax.axis_index("row"), lax.axis_index("col"), lax.axis_index("depth")
    z, x = row // NX, lax.rem(row, NX)

    def zz(k):
        return lax.rem(z + (k % NZ), NZ)

    def xx(k):
        return lax.rem(x + (k % NX), NX)

    def yy(k):
        return lax.rem(y + (k % NY), NY)

    zp, zm = (zz(1) * NX + x, c, y), (zz(-1) * NX + x, c, y)
    xp, xm = (z * NX + xx(1), c, y), (z * NX + xx(-1), c, y)
    yp, ym, y2 = (row, c, yy(1)), (row, c, yy(-1)), (row, c, yy(2))
    core = (row, 1 - c, y)
    started = []

    def push(src, dst, dev):
        k = len(started)
        copy = pltpu.make_async_remote_copy(
            src_ref=src, dst_ref=dst, send_sem=send.at[k], recv_sem=recv.at[k], device_id=dev, device_id_type=MESH
        )
        copy.start()
        started.append(copy)
        return copy

    Wp[z, x, :, 0:MAIN] = w[:, 0:MAIN]
    Wp[z, x, :, MAIN:WIDE] = w[:, pl.ds(pl.multiple_of(MAIN + TILE * y, TILE), TILE)]

    barrier = pltpu.get_barrier_semaphore()
    for dev in (zp, zm, xp, xm, yp, ym, y2, core):
        pl.semaphore_signal(barrier, inc=1, device_id=dev, device_id_type=MESH)
    pl.semaphore_wait(barrier, 8)

    def ablk(k, h, r0, n):
        return A.at[pl.ds(pl.multiple_of(yy(k) * TOK + r0, 128), n), pl.ds(pl.multiple_of(h * HALF, 128), HALF)]

    HT = TOK // 2
    wz, wx, wr, wy = {}, {}, {}, {}

    def blk(k, r0, n):
        return Wp.at[zz(k), x, pl.ds(r0, n), :]

    def pushz(step):
        k = step - 1
        if step < 4:
            wz[step, 0] = push(blk(-k, 0, R1), blk(-k, 0, R1), zp)
            wz[step, 1] = push(blk(k, 0, R1), blk(k, 0, R1), zm)
        else:
            wz[step, 0] = push(blk(-k, 0, R1 // 2), blk(-k, 0, R1 // 2), zp)
            wz[step, 1] = push(blk(k, R1 // 2, R1 // 2), blk(k, R1 // 2, R1 // 2), zm)

    def waitz(step):
        wz[step, 0].wait_recv()
        wz[step, 1].wait_recv()

    def pushx(k):
        wx[k, 0] = push(blk(k, 0, R1), blk(k, 0, R1), xp)
        wx[k, 1] = push(blk(k, 0, R1), blk(k, 0, R1), xm)

    def relayx(k):
        h = R1 // 2
        wx[k, 0].wait_recv()
        left = Wp.at[zz(k), xx(-1), pl.ds(0, h), :]
        wx[k, 2] = push(left, left, xp)
        wx[k, 1].wait_recv()
        right = Wp.at[zz(k), xx(1), pl.ds(h, h), :]
        wx[k, 3] = push(right, right, xm)

    def waitx(k):
        wx[k, 2].wait_recv()
        wx[k, 3].wait_recv()

    R2 = BLK - R1

    def rblk(k, r0, n):
        return Wp.at[zz(k), :, pl.ds(r0, n), :]

    def pushr(step):
        k = step - 1
        if step < 4:
            wr[step, 0] = push(rblk(-k, R1, R2), rblk(-k, R1, R2), zp)
            wr[step, 1] = push(rblk(k, R1, R2), rblk(k, R1, R2), zm)
        else:
            h = R2 // 2
            wr[step, 0] = push(rblk(-k, R1, h), rblk(-k, R1, h), zp)
            wr[step, 1] = push(rblk(k, R1 + h, h), rblk(k, R1 + h, h), zm)

    def waitr(step):
        wr[step, 0].wait_recv()
        wr[step, 1].wait_recv()

    def wtile(k, j):
        return Wr.at[zz(k), :, :, pl.ds(j * TILE, TILE)]

    def pushy(k):
        src = Wp.at[zz(k), :, :, pl.ds(MAIN, TILE)]
        wy[k, 0] = push(src, wtile(k, 0), yp)
        wy[k, 1] = push(src, wtile(k, 1), ym)

    def relayy(k):
        if k % 2 == 0:
            wy[k, 0].wait_recv()
            wy[k, 2] = push(wtile(k, 0), wtile(k, 2), yp)
        else:
            wy[k, 1].wait_recv()
            wy[k, 2] = push(wtile(k, 1), wtile(k, 2), ym)

    def waity(k):
        wy[k, 1 - k % 2].wait_recv()
        wy[k, 2].wait_recv()

    pushz(1)
    X1 = Wp.at[z, x, pl.ds(R1, R2), :]
    wxr = [push(X1, X1, xp), push(X1, X1, xm)]
    at = {}
    at["ap"] = push(attn.at[pl.ds(0, HT)], ablk(0, c, 0, HT), yp)
    at["bm"] = push(attn.at[pl.ds(HT, HT)], ablk(0, c, HT, HT), ym)
    pushx(0)
    at["bp"] = push(attn.at[pl.ds(HT, HT)], ablk(0, c, HT, HT), yp)
    at["am"] = push(attn.at[pl.ds(0, HT)], ablk(0, c, 0, HT), ym)
    ct = []
    for k, dev in ((1, yp), (-1, ym), (2, y2)):
        q = cot.at[:, pl.ds(pl.multiple_of(yy(k) * QUART, 128), QUART)]
        ct.append(push(q, CQ.at[pl.ds(pl.multiple_of(y * TOK, TOK), TOK), :], dev))
    cc = [push(attn, ablk(0, c, 0, TOK), core)]
    A[pl.ds(pl.multiple_of(y * TOK, TOK), TOK), pl.ds(pl.multiple_of(c * HALF, 128), HALF)] = attn[...]
    CQ[pl.ds(pl.multiple_of(y * TOK, TOK), TOK), :] = cot[:, pl.ds(pl.multiple_of(y * QUART, 128), QUART)]
    cotp[:, 0:MAIN] = cot[:, 0:MAIN]
    for j, k in enumerate((0, -1, 1, 2)):
        cotp[:, MAIN + j * TILE:MAIN + (j + 1) * TILE] = cot[:, pl.ds(pl.multiple_of(MAIN + yy(k) * TILE, TILE), TILE)]

    waitz(1)
    pushz(2)
    pushx(-1)
    pushx(1)
    wxr[0].wait_recv()
    h = R2 // 2
    left = Wp.at[z, xx(-1), pl.ds(R1, h), :]
    wxr.append(push(left, left, xp))
    wxr[1].wait_recv()
    right = Wp.at[z, xx(1), pl.ds(R1 + h, h), :]
    wxr.append(push(right, right, xm))
    relayx(0)
    waitz(2)
    pushz(3)
    pushx(-2)
    pushx(2)
    at["ap"].wait_recv()
    at["rp"] = push(ablk(-1, c, 0, HT), ablk(-1, c, 0, HT), yp)
    at["bm"].wait_recv()
    at["rm"] = push(ablk(1, c, HT, HT), ablk(1, c, HT, HT), ym)
    wxr[2].wait_recv()
    wxr[3].wait_recv()
    pushr(1)
    waitz(3)
    pushz(4)
    pushx(-3)
    pushx(3)
    relayx(-1)
    relayx(1)
    waitr(1)
    pushr(2)
    at["bp"].wait_recv()
    cc.append(push(ablk(-1, c, 0, TOK), ablk(-1, c, 0, TOK), core))
    at["am"].wait_recv()
    cc.append(push(ablk(1, c, 0, TOK), ablk(1, c, 0, TOK), core))
    waitz(4)
    pushx(4)
    waitx(0)
    pushy(0)
    relayx(-2)
    relayx(2)
    waitr(2)
    pushr(3)
    relayx(-3)
    relayx(3)
    waitr(3)
    pushr(4)
    for copy in ct:
        copy.wait_recv()
    at["rp"].wait_recv()
    at["rm"].wait_recv()
    cc.append(push(ablk(2, c, 0, TOK), ablk(2, c, 0, TOK), core))
    waitx(-1)
    pushy(-1)
    waitx(1)
    pushy(1)
    relayx(4)
    for copy in cc:
        copy.wait_recv()

    def term(k):
        zi = zz(k)
        a = A[:, pl.ds(pl.multiple_of(zi * NX * BLK, 128), NX * BLK)]
        g = lax.dot_general(a, CQ[...], (((0,), (0,)), ((), ())), preferred_element_type=F32)
        G[zi] = g.reshape(NX, BLK, QUART)

    H1 = S1 // 2
    S2 = BLK - S1
    H2 = S2 // 2
    M2 = S1 + H2
    gx, gz, gy, gyx = {}, {}, {}, {}

    def sumx1(k):
        gx[k, 0] = push(G.at[zz(k), xx(2), pl.ds(0, H1)], xa.at[k % NZ, 0], xp)
        gx[k, 1] = push(G.at[zz(k), xx(2), pl.ds(H1, H1)], xa.at[k % NZ, 1], xm)

    def sumx2(k):
        gx[k, 0].wait_recv()
        G[zz(k), xx(1), 0:H1] += xa[k % NZ, 0]
        gx[k, 2] = push(G.at[zz(k), xx(1), pl.ds(0, S1)], xb.at[k % NZ, 0], xp)
        gx[k, 1].wait_recv()
        G[zz(k), xx(-1), H1:S1] += xa[k % NZ, 1]
        gx[k, 3] = push(G.at[zz(k), xx(-1), pl.ds(0, S1)], xb.at[k % NZ, 1], xm)

    def sumx3(k):
        gx[k, 2].wait_recv()
        gx[k, 3].wait_recv()
        G[zz(k), x, 0:S1] += xb[k % NZ, 0] + xb[k % NZ, 1]

    def sumz(step):
        if step == 1:
            gz[1, 0] = push(G.at[zz(4), x, pl.ds(0, H1)], za4.at[0], zp)
            gz[1, 1] = push(G.at[zz(4), x, pl.ds(H1, H1)], za4.at[1], zm)
            return
        gz[step - 1, 0].wait_recv()
        gz[step - 1, 1].wait_recv()
        if step == 2:
            G[zz(3), x, 0:H1] += za4[0]
            G[zz(-3), x, H1:S1] += za4[1]
        elif step < 5:
            G[zz(5 - step), x, 0:S1] += za[step - 3, 0]
            G[zz(step - 5), x, 0:S1] += za[step - 3, 1]
        else:
            G[z, x, 0:S1] += za[2, 0] + za[2, 1]
            return
        gz[step, 0] = push(G.at[zz(5 - step), x, pl.ds(0, S1)], za.at[step - 2, 0], zp)
        gz[step, 1] = push(G.at[zz(step - 5), x, pl.ds(0, S1)], za.at[step - 2, 1], zm)

    def sumy(step):
        if step == 1:
            gy[1, 0] = push(G.at[zz(4), :, pl.ds(S1, H2)], yb.at[0], zp)
            gy[1, 1] = push(G.at[zz(4), :, pl.ds(M2, H2)], yb.at[1], zm)
            return
        gy[step - 1, 0].wait_recv()
        gy[step - 1, 1].wait_recv()
        if step == 2:
            G[zz(3), :, S1:M2] += yb[0]
            G[zz(-3), :, M2:BLK] += yb[1]
        elif step < 5:
            G[zz(5 - step), :, S1:BLK] += ya[step - 3, 0]
            G[zz(step - 5), :, S1:BLK] += ya[step - 3, 1]
        else:
            G[z, :, S1:BLK] += ya[2, 0] + ya[2, 1]
            return
        gy[step, 0] = push(G.at[zz(5 - step), :, pl.ds(S1, S2)], ya.at[step - 2, 0], zp)
        gy[step, 1] = push(G.at[zz(step - 5), :, pl.ds(S1, S2)], ya.at[step - 2, 1], zm)

    def fwd(lo, width, src, at_col):
        a = A[pl.ds(pl.multiple_of(y * TOK, TOK), TOK), :]
        p = jnp.dot(a, src[:, :, :, lo:lo + width].reshape(NZ * NX * BLK, width), preferred_element_type=F32)
        proj[:, pl.ds(at_col, width)] = p.astype(BF16)

    def col(k):
        return pl.multiple_of(MAIN + yy(k) * TILE, TILE)

    def bwd(zi):
        return lax.dot_general(
            cotp[:, 0:WIDE], Wp[zi].reshape(NX * BLK, WIDE), (((1,), (1,)), ((), ())), preferred_element_type=F32
        )

    def bwd_rest(zi):
        return lax.dot_general(
            cotp[:, WIDE:], Wr[zi].reshape(NX * BLK, HALF - WIDE), (((1,), (1,)), ((), ())), preferred_element_type=F32
        )

    term(4)
    sumy(1)
    sumx1(4)
    term(3)
    sumx1(3)
    term(-3)
    sumx1(-3)
    term(2)
    term(-2)
    waitr(4)
    waitx(-2)
    pushy(-2)
    waitx(2)
    pushy(2)
    waitx(-3)
    pushy(-3)
    waitx(3)
    pushy(3)
    waitx(4)
    pushy(4)
    sumx2(4)
    sumy(2)
    sumx1(2)
    sumx1(-2)
    term(1)
    term(-1)
    sumx2(3)
    sumx2(-3)
    sumx1(1)
    sumx1(-1)
    relayy(0)
    relayy(-1)
    relayy(1)
    term(0)
    sumx3(4)
    sumz(1)
    fwd(0, 256, Wp, 0)
    sumx1(0)
    sumy(3)
    sumx2(2)
    sumx2(-2)
    sumx3(3)
    sumx3(-3)
    sumz(2)
    relayy(-2)
    relayy(2)
    fwd(256, 256, Wp, 256)
    fwd(512, 256, Wp, 512)
    sumx2(1)
    sumx2(-1)
    sumy(4)
    sumx3(2)
    sumx3(-2)
    sumz(3)
    relayy(-3)
    relayy(3)
    fwd(768, 256, Wp, 768)
    fwd(MAIN, TILE, Wp, col(0))
    sumx2(0)
    sumx3(1)
    sumx3(-1)
    sumz(4)
    relayy(4)
    for j in range(4):
        bo[j] = bwd(4 * (1 - c) + j)
    sumy(5)
    gyx[0] = push(G.at[z, xx(2), pl.ds(S1, H2)], yxa.at[0], xp)
    gyx[1] = push(G.at[z, xx(2), pl.ds(M2, H2)], yxa.at[1], xm)
    for j in range(4):
        bm[j] = bwd(4 * c + j)
    gyx[0].wait_recv()
    G[z, xx(1), S1:M2] += yxa[0]
    gyx[2] = push(G.at[z, xx(1), pl.ds(S1, S2)], yxb.at[0], xp)
    gyx[1].wait_recv()
    G[z, xx(-1), M2:BLK] += yxa[1]
    gyx[3] = push(G.at[z, xx(-1), pl.ds(S1, S2)], yxb.at[1], xm)
    sumx3(0)
    sumz(5)
    scale = 1.0 / math.sqrt(TOK * NZ * NX * NY)
    mine = pl.ds(pl.multiple_of(y * QUART, 128), QUART)
    wgrad[0:S1, mine] = G[z, x, 0:S1] * scale
    last = [push(wgrad.at[pl.ds(0, S1), mine], wgrad.at[pl.ds(0, S1), mine], dev) for dev in (yp, ym, y2)]
    gyx[2].wait_recv()
    gyx[3].wait_recv()
    wgrad[S1:BLK, mine] = (G[z, x, S1:BLK] + (yxb[0] + yxb[1])) * scale
    last += [push(wgrad.at[pl.ds(S1, S2), mine], wgrad.at[pl.ds(S1, S2), mine], dev) for dev in (yp, ym, y2)]
    for k in (0, -1, 1, -2, 2, -3, 3, 4):
        waity(k)
    back = []
    for j in range(4):
        bo[j] += bwd_rest(4 * (1 - c) + j)
        back.append(push(bo.at[j], br.at[j], core))
    for j in range(4):
        bm[j] += bwd_rest(4 * c + j)
    for j, k in enumerate((-1, 1, 2)):
        fwd(j * TILE, TILE, Wr, col(k))
    for j in range(4):
        back[j].wait_recv()
        igrad[:, j * NX * BLK:(j + 1) * NX * BLK] = (bm[j] + br[j]).astype(BF16)
    for copy in last:
        copy.wait_recv()
    for copy in started:
        copy.wait_send()


def body(attn, w, cot):
    h1, s2, h2 = S1 // 2, BLK - S1, (BLK - S1) // 2
    vmem = pl.BlockSpec(memory_space=pltpu.VMEM)
    return pl.pallas_call(
        kernel,
        out_shape=(
            jax.ShapeDtypeStruct((TOK, HALF), BF16),
            jax.ShapeDtypeStruct((TOK, HALF), BF16),
            jax.ShapeDtypeStruct((BLK, HALF), F32),
        ),
        in_specs=[vmem] * 3,
        out_specs=(vmem,) * 3,
        scratch_shapes=[
            pltpu.VMEM((NY * TOK, 2 * HALF), BF16),
            pltpu.VMEM((NY * TOK, QUART), BF16),
            pltpu.VMEM((NZ, NX, BLK, WIDE), BF16),
            pltpu.VMEM((NZ, NX, BLK, HALF - WIDE), BF16),
            pltpu.VMEM((TOK, HALF), BF16),
            pltpu.VMEM((NZ, NX, BLK, QUART), F32),
            pltpu.VMEM((4, TOK, NX * BLK), F32),
            pltpu.VMEM((4, TOK, NX * BLK), F32),
            pltpu.VMEM((4, TOK, NX * BLK), F32),
            pltpu.VMEM((NZ, 2, h1, QUART), F32),
            pltpu.VMEM((NZ, 2, S1, QUART), F32),
            pltpu.VMEM((3, 2, S1, QUART), F32),
            pltpu.VMEM((2, h1, QUART), F32),
            pltpu.VMEM((2, h1, QUART), F32),
            pltpu.VMEM((3, 2, NX, s2, QUART), F32),
            pltpu.VMEM((2, NX, h2, QUART), F32),
            pltpu.VMEM((2, h2, QUART), F32),
            pltpu.VMEM((2, s2, QUART), F32),
            pltpu.SemaphoreType.DMA((N_MSG,)),
            pltpu.SemaphoreType.DMA((N_MSG,)),
        ],
        compiler_params=pltpu.CompilerParams(
            collective_id=0, has_side_effects=True, vmem_limit_bytes=56 * 2**20
        ),
        name="projection",
    )(attn, w, cot)


def solution(mesh):
    in_specs = (P(("depth", "row"), "col"), P("row", "col"), P(("depth", "row"), "col"))
    out_specs = (P(("depth", "row"), "col"), P(("depth", "row"), "col"), P("row", "col"))
    return jax.shard_map(body, mesh=mesh, in_specs=in_specs, out_specs=out_specs, check_vma=False)
```

time: 465 us -> 109 us (0.23)
  waiting for transfers between devices: 420 us -> 0 us
  Pallas kernels: 0 us -> 103 us
  matrix products: 24.7 us -> 0 us
  between operations: 13.8 us -> 0.65 us
    reduce_scatter x2 -> x0, waiting for transfers between devices: 253 us -> none  [the longest x1 243 us: body(): lax.psum_scatter(lax.dot_general(columns, cotangent, (((0,), (0,)), ((),...]
    all_gather x2 -> x0, waiting for transfers between devices: 117 us -> none  [the longest x1 97.9 us: body(): lax.all_gather(w_out, 'row', axis=0, tiled=True)]
    pallas_call x0 -> x1, Pallas kernels: none -> 103 us  [body(): pl.pallas_call(kernel, out_shape=(jax.ShapeDtypeStruct((TOK, HALF), BF16)...]
    psum x1 -> x0, waiting for transfers between devices: 48.9 us -> none  [body(): total = lax.psum(row_summed, 'depth')]
    dot_general x3 -> x0, matrix products: 24.7 us -> none  [the longest x1 9.44 us: body(): lax.dot_general(columns, cotangent, (((0,), (0,)), ((), ())), preferred_e...]
  transfers between devices with their start and end apart: 5 -> 0, of which waited for: 5 -> 0; matrix products, arithmetic and copies ran while one was open for 6% -> 0% of each run, Pallas kernels for 0% -> 0%
where the time goes in v1:
time: 109 us; the launch traced here: 108 us
  Pallas kernels  103 us (94%)
  local copies, waits for them, and re-layouts  4.3 us (4%)
    pallas_call x1, Pallas kernels, body(): pl.pallas_call(kernel, out_shape=(jax.ShapeDtypeStruct((TOK, HALF), BF16)...  103 us
    unnamed x7, local copies, waits for them, and re-layouts  4.3 us

profile of v1, /device:TPU:16, one launch (start us, length us, event | category | flops | bytes accessed | tf_op | source)
XLA Modules:
  0.0 107.5 jit_solution(13368288582410829327)
XLA Ops:
  0.6 102.6 %projection.1 = (bf16[256,1536]{1,0:T(8,128)(2,1)}, bf16[256,1536]{1,0:T(8,128)(2,1)}, f32[96,1536]{1,0:T(8,128)}) custom-call(bf16[256,1536]{1,0:T(8,128)(2,1)} %attn.1, bf16[96,1536]{1,0:T(8,128)(2,1)} %w.1, bf16[256,1536]{1,0:T(8,128)(2,1)} %cot.1), custom_call_target="tpu_custom_call" | custom-call | tf_op jit(solution)/shard_map/projection/pallas_call | solution.py:410
  103.2 0.0 copy-start
  103.2 2.1 %copy.9 = bf16[256,1536]{1,0:T(8,128)(2,1)} copy(bf16[256,1536]{1,0:T(8,128)(2,1)} %get-tuple-element.6) | data formatting | bytes 1572864
  105.4 0.0 copy-done
  105.4 0.0 copy-start.1
  105.4 0.9 copy.10
  106.2 0.5 copy-done.1
  106.7 0.8 copy.11
Async XLA Ops:
  103.2 2.1 %copy-start = (bf16[256,1536]{1,0:T(8,128)(2,1)S(1)}, bf16[256,1536]{1,0:T(8,128)(2,1)}, u32[]{:S(2)}) copy-start(bf16[256,1536]{1,0:T(8,128)(2,1)} %get-tuple-element.7) | copy-start | bytes 2359300
  105.4 1.3 %copy-start.1 = (f32[96,1536]{1,0:T(8,128)S(1)}, f32[96,1536]{1,0:T(8,128)}, u32[]{:S(2)}) copy-start(f32[96,1536]{1,0:T(8,128)} %get-tuple-element.8) | copy-start | bytes 1769476

commit v2 on v0

v2 whole, which is shorter than its diff:
```python
import math

import jax
import jax.numpy as jnp
from jax import lax
from jax.experimental import pallas as pl
from jax.experimental.pallas import tpu as pltpu
from jax.sharding import PartitionSpec as P

MESH = pl.DeviceIdType.MESH
NZ, NX, NY = 8, 4, 4
TOK, HALF, BLK = 256, 1536, 96
MAIN, TILE = 1024, 128
WIDE = MAIN + TILE
QUART = HALF // NY
R1 = 64
R2 = BLK - R1
S1 = 48
S2 = BLK - S1
H1, H2 = S1 // 2, S2 // 2
M2 = S1 + H2
HT = TOK // 2
ZBLK = NX * BLK
F32, BF16 = jnp.float32, jnp.bfloat16
N_MSG = 208


def kernel(attn, w, cot, proj, igrad, wgrad, A, CQ, Wp, Wr, cotp, G, bo, bm, br,
           xa, xb, za, za4, ya, yb, yxa, yxb, send, recv):
    row, c, y = lax.axis_index("row"), lax.axis_index("col"), lax.axis_index("depth")
    z, x = row // NX, lax.rem(row, NX)

    def zz(k):
        return lax.rem(z + (k % NZ), NZ)

    def xx(k):
        return lax.rem(x + (k % NX), NX)

    def yy(k):
        return lax.rem(y + (k % NY), NY)

    zp, zm = (zz(1) * NX + x, c, y), (zz(-1) * NX + x, c, y)
    xp, xm = (z * NX + xx(1), c, y), (z * NX + xx(-1), c, y)
    yp, ym, y2 = (row, c, yy(1)), (row, c, yy(-1)), (row, c, yy(2))
    core = (row, 1 - c, y)
    started = []

    def push(src, dst, dev):
        k = len(started)
        copy = pltpu.make_async_remote_copy(
            src_ref=src, dst_ref=dst, send_sem=send.at[k], recv_sem=recv.at[k], device_id=dev, device_id_type=MESH
        )
        copy.start()
        started.append(copy)
        return copy

    def same(ref, dev):
        return push(ref, ref, dev)

    at, ct, cc, wz, wx, wr, wxr, wy = {}, {}, {}, {}, {}, {}, {}, {}
    gx, gz, gy, gyx, last, back = {}, {}, {}, {}, {}, {}

    def ablk(k, h, r0, n):
        return A.at[pl.ds(pl.multiple_of(yy(k) * TOK + r0, 128), n), pl.ds(pl.multiple_of(h * HALF, 128), HALF)]

    def att(i):
        r0 = i * HT
        at[i, 0] = push(attn.at[pl.ds(r0, HT)], ablk(0, c, r0, HT), yp)
        r0 = (1 - i) * HT
        at[i, 1] = push(attn.at[pl.ds(r0, HT)], ablk(0, c, r0, HT), ym)

    def att_on(i):
        at[0, i].wait_recv()
        k = -1 if i == 0 else 1
        at[2, i] = same(ablk(k, c, i * HT, HT), yp if i == 0 else ym)

    def cots(k):
        q = cot.at[:, pl.ds(pl.multiple_of(yy(k) * QUART, 128), QUART)]
        ct[k] = push(q, CQ.at[pl.ds(pl.multiple_of(y * TOK, TOK), TOK), :], {1: yp, -1: ym, 2: y2}[k])

    def cots_in():
        for k in (1, -1, 2):
            ct[k].wait_recv()

    def own():
        cc[0] = push(attn, ablk(0, c, 0, TOK), core)
        A[pl.ds(pl.multiple_of(y * TOK, TOK), TOK), pl.ds(pl.multiple_of(c * HALF, 128), HALF)] = attn[...]
        CQ[pl.ds(pl.multiple_of(y * TOK, TOK), TOK), :] = cot[:, pl.ds(pl.multiple_of(y * QUART, 128), QUART)]
        cotp[:, 0:MAIN] = cot[:, 0:MAIN]
        for j, k in enumerate((0, -1, 1, 2)):
            lane = pl.multiple_of(MAIN + yy(k) * TILE, TILE)
            cotp[:, MAIN + j * TILE:MAIN + (j + 1) * TILE] = cot[:, pl.ds(lane, TILE)]

    def cross(k):
        if k == 2:
            at[2, 0].wait_recv()
            at[2, 1].wait_recv()
        else:
            at[1, 0 if k == -1 else 1].wait_recv()
        cc[k] = same(ablk(k, c, 0, TOK), core)

    def cross_in(k):
        cc[k].wait_recv()

    def blk(k, r0, n):
        return Wp.at[zz(k), x, pl.ds(r0, n), :]

    def zpush(step):
        k, h = step - 1, R1 // 2
        if step < 4:
            wz[step, 0] = same(blk(-k, 0, R1), zp)
            wz[step, 1] = same(blk(k, 0, R1), zm)
        else:
            wz[step, 0] = same(blk(-k, 0, h), zp)
            wz[step, 1] = same(blk(k, h, h), zm)

    def zstep(step):
        wz[step, 0].wait_recv()
        wz[step, 1].wait_recv()
        if step < 4:
            zpush(step + 1)

    def xpush(k):
        wx[k, 0] = same(blk(k, 0, R1), xp)
        wx[k, 1] = same(blk(k, 0, R1), xm)

    def xstep(k):
        h = R1 // 2
        wx[k, 0].wait_recv()
        wx[k, 2] = same(Wp.at[zz(k), xx(-1), pl.ds(0, h), :], xp)
        wx[k, 1].wait_recv()
        wx[k, 3] = same(Wp.at[zz(k), xx(1), pl.ds(h, h), :], xm)

    def xlast(k):
        wx[k, 2].wait_recv()
        wx[k, 3].wait_recv()

    def rx():
        mine = Wp.at[z, x, pl.ds(R1, R2), :]
        wxr[0] = same(mine, xp)
        wxr[1] = same(mine, xm)

    def rx_on():
        h = R2 // 2
        wxr[0].wait_recv()
        wxr[2] = same(Wp.at[z, xx(-1), pl.ds(R1, h), :], xp)
        wxr[1].wait_recv()
        wxr[3] = same(Wp.at[z, xx(1), pl.ds(R1 + h, h), :], xm)

    def rx_in():
        wxr[2].wait_recv()
        wxr[3].wait_recv()

    def rpush(step, j):
        k, h = step - 1, R2 // 2
        if step < 4:
            wr[step, j, 0] = same(Wp.at[zz(-k), xx(j), pl.ds(R1, R2), :], zp)
            wr[step, j, 1] = same(Wp.at[zz(k), xx(j), pl.ds(R1, R2), :], zm)
        else:
            wr[step, j, 0] = same(Wp.at[zz(-k), xx(j), pl.ds(R1, h), :], zp)
            wr[step, j, 1] = same(Wp.at[zz(k), xx(j), pl.ds(R1 + h, h), :], zm)

    def rstep(step, j):
        wr[step, j, 0].wait_recv()
        wr[step, j, 1].wait_recv()
        if step < 4:
            rpush(step + 1, j)

    def wtile(k, j):
        return Wr.at[zz(k), :, :, pl.ds(j * TILE, TILE)]

    def ypush(k):
        src = Wp.at[zz(k), :, :, pl.ds(MAIN, TILE)]
        wy[k, 0] = push(src, wtile(k, 0), yp)
        wy[k, 1] = push(src, wtile(k, 1), ym)

    def ystep(k):
        j = k % 2
        wy[k, j].wait_recv()
        wy[k, 2] = push(wtile(k, j), wtile(k, 2), ym if j else yp)

    def ylast(k):
        wy[k, 1 - k % 2].wait_recv()
        wy[k, 2].wait_recv()

    def term(k):
        zi = zz(k)
        a = A[:, pl.ds(pl.multiple_of(zi * ZBLK, 128), ZBLK)]
        g = lax.dot_general(a, CQ[...], (((0,), (0,)), ((), ())), preferred_element_type=F32)
        G[zi] = g.reshape(NX, BLK, QUART)

    def sumx(k):
        gx[k, 0] = push(G.at[zz(k), xx(2), pl.ds(0, H1)], xa.at[k % NZ, 0], xp)
        gx[k, 1] = push(G.at[zz(k), xx(2), pl.ds(H1, H1)], xa.at[k % NZ, 1], xm)

    def sumx_on(k):
        gx[k, 0].wait_recv()
        G[zz(k), xx(1), 0:H1] += xa[k % NZ, 0]
        gx[k, 2] = push(G.at[zz(k), xx(1), pl.ds(0, S1)], xb.at[k % NZ, 0], xp)
        gx[k, 1].wait_recv()
        G[zz(k), xx(-1), H1:S1] += xa[k % NZ, 1]
        gx[k, 3] = push(G.at[zz(k), xx(-1), pl.ds(0, S1)], xb.at[k % NZ, 1], xm)

    def sumx_in(k):
        gx[k, 2].wait_recv()
        gx[k, 3].wait_recv()
        G[zz(k), x, 0:S1] += xb[k % NZ, 0] + xb[k % NZ, 1]

    def sumz(step):
        if step == 1:
            gz[1, 0] = push(G.at[zz(4), x, pl.ds(0, H1)], za4.at[0], zp)
            gz[1, 1] = push(G.at[zz(4), x, pl.ds(H1, H1)], za4.at[1], zm)
            return
        gz[step - 1, 0].wait_recv()
        gz[step - 1, 1].wait_recv()
        if step == 2:
            G[zz(3), x, 0:H1] += za4[0]
            G[zz(-3), x, H1:S1] += za4[1]
        elif step < 5:
            G[zz(5 - step), x, 0:S1] += za[step - 3, 0]
            G[zz(step - 5), x, 0:S1] += za[step - 3, 1]
        else:
            G[z, x, 0:S1] += za[2, 0] + za[2, 1]
            return
        gz[step, 0] = push(G.at[zz(5 - step), x, pl.ds(0, S1)], za.at[step - 2, 0], zp)
        gz[step, 1] = push(G.at[zz(step - 5), x, pl.ds(0, S1)], za.at[step - 2, 1], zm)

    def sumy(step, j):
        i, d = xx(j), j % NX
        if step == 1:
            gy[1, j, 0] = push(G.at[zz(4), i, pl.ds(S1, H2)], yb.at[0, d], zp)
            gy[1, j, 1] = push(G.at[zz(4), i, pl.ds(M2, H2)], yb.at[1, d], zm)
            return
        gy[step - 1, j, 0].wait_recv()
        gy[step - 1, j, 1].wait_recv()
        if step == 2:
            G[zz(3), i, S1:M2] += yb[0, d]
            G[zz(-3), i, M2:BLK] += yb[1, d]
        elif step < 5:
            G[zz(5 - step), i, S1:BLK] += ya[step - 3, 0, d]
            G[zz(step - 5), i, S1:BLK] += ya[step - 3, 1, d]
        else:
            G[z, i, S1:BLK] += ya[2, 0, d] + ya[2, 1, d]
            return
        gy[step, j, 0] = push(G.at[zz(5 - step), i, pl.ds(S1, S2)], ya.at[step - 2, 0, d], zp)
        gy[step, j, 1] = push(G.at[zz(step - 5), i, pl.ds(S1, S2)], ya.at[step - 2, 1, d], zm)

    def sumyx():
        gyx[0] = push(G.at[z, xx(2), pl.ds(S1, H2)], yxa.at[0], xp)
        gyx[1] = push(G.at[z, xx(2), pl.ds(M2, H2)], yxa.at[1], xm)

    def sumyx_on():
        gyx[0].wait_recv()
        G[z, xx(1), S1:M2] += yxa[0]
        gyx[2] = push(G.at[z, xx(1), pl.ds(S1, S2)], yxb.at[0], xp)
        gyx[1].wait_recv()
        G[z, xx(-1), M2:BLK] += yxa[1]
        gyx[3] = push(G.at[z, xx(-1), pl.ds(S1, S2)], yxb.at[1], xm)

    def wout(r0, n, g):
        at_y = pl.ds(pl.multiple_of(y * QUART, 128), QUART)
        wgrad[r0:r0 + n, at_y] = g * (1.0 / math.sqrt(TOK * NZ * NX * NY))
        for dev in (yp, ym, y2):
            last[len(last)] = same(wgrad.at[pl.ds(r0, n), at_y], dev)

    def wout_x():
        wout(0, S1, G[z, x, 0:S1])

    def wout_y():
        gyx[2].wait_recv()
        gyx[3].wait_recv()
        wout(S1, S2, G[z, x, S1:BLK] + (yxb[0] + yxb[1]))

    def fwd(src, lo, width, at_col):
        a = A[pl.ds(pl.multiple_of(y * TOK, TOK), TOK), :]
        p = jnp.dot(a, src[:, :, :, lo:lo + width].reshape(NZ * ZBLK, width), preferred_element_type=F32)
        proj[:, pl.ds(at_col, width)] = p.astype(BF16)

    def lane(k):
        return pl.multiple_of(MAIN + yy(k) * TILE, TILE)

    def fwd_main(n):
        if n < 4:
            fwd(Wp, 256 * n, 256, 256 * n)
        else:
            fwd(Wp, MAIN, TILE, lane(0))

    def fwd_rest(n):
        fwd(Wr, n * TILE, TILE, lane((-1, 1, 2)[n]))

    def bwd(ref, cols, zi):
        wide = ref.shape[-1]
        return lax.dot_general(
            cols, ref[zi].reshape(ZBLK, wide), (((1,), (1,)), ((), ())), preferred_element_type=F32
        )

    def bwd_other(j):
        bo[j] = bwd(Wp, cotp[:, 0:WIDE], 4 * (1 - c) + j)

    def bwd_own(j):
        bm[j] = bwd(Wp, cotp[:, 0:WIDE], 4 * c + j)

    def bwd_send(j):
        bo[j] += bwd(Wr, cotp[:, WIDE:], 4 * (1 - c) + j)
        back[j] = push(bo.at[j], br.at[j], core)

    def bwd_rest(j):
        bm[j] += bwd(Wr, cotp[:, WIDE:], 4 * c + j)

    def bwd_out(j):
        back[j].wait_recv()
        igrad[:, j * ZBLK:(j + 1) * ZBLK] = (bm[j] + br[j]).astype(BF16)

    Wp[z, x, :, 0:MAIN] = w[:, 0:MAIN]
    Wp[z, x, :, MAIN:WIDE] = w[:, pl.ds(pl.multiple_of(MAIN + TILE * y, TILE), TILE)]
    barrier = pltpu.get_barrier_semaphore()
    for dev in (zp, zm, xp, xm, yp, ym, y2, core):
        pl.semaphore_signal(barrier, inc=1, device_id=dev, device_id_type=MESH)
    pl.semaphore_wait(barrier, 8)

    att(0)
    rx()
    att(1)
    zpush(1)
    rpush(1, 0)
    xpush(0)
    own()
    rx_on()
    rpush(1, -1)
    rpush(1, 1)
    zstep(1)
    xpush(-1)
    xpush(1)
    xstep(0)
    rstep(1, 0)
    cross_in(0)
    rx_in()
    rpush(1, 2)
    cots(1)
    cots(-1)
    rstep(1, -1)
    rstep(1, 1)
    xstep(-1)
    att_on(0)
    att_on(1)
    zstep(2)
    xpush(2)
    xpush(-2)
    xstep(1)
    rstep(2, 0)
    xlast(0)
    rstep(1, 2)
    xlast(-1)
    rstep(2, -1)
    cross(-1)
    cross(1)
    rstep(2, 1)
    xstep(2)
    ypush(-1)
    zstep(3)
    xpush(-3)
    cots(2)
    xpush(3)
    xstep(-2)
    rstep(3, 0)
    cross_in(-1)
    xlast(1)
    ypush(1)
    rstep(2, 2)
    xlast(2)
    ypush(2)
    rstep(3, -1)
    cross_in(1)
    rstep(3, 1)
    ypush(0)
    xstep(-3)
    zstep(4)
    xpush(4)
    cross(2)
    rstep(4, 0)
    xstep(3)
    rstep(3, 2)
    ystep(-1)
    rstep(4, -1)
    xlast(-2)
    ypush(-2)
    rstep(4, 1)
    rstep(4, 2)
    cots_in()
    xlast(-3)
    ypush(-3)
    cross_in(2)
    term(4)
    sumy(1, 2)
    sumy(1, -1)
    sumy(1, 0)
    sumx(4)
    ystep(1)
    term(-3)
    sumy(1, 1)
    ystep(2)
    term(3)
    xlast(3)
    sumx(3)
    sumy(2, 2)
    sumx(-3)
    term(-2)
    ystep(0)
    sumx_on(4)
    sumx(-2)
    sumy(2, -1)
    sumy(2, 1)
    term(2)
    sumx(2)
    ystep(-2)
    ylast(-1)
    sumx_on(-3)
    sumy(3, 2)
    sumx_on(3)
    xstep(4)
    term(1)
    sumx_in(4)
    sumz(1)
    sumy(3, -1)
    term(-1)
    ypush(3)
    sumx(1)
    sumx_on(2)
    term(0)
    ystep(-3)
    ylast(2)
    sumy(3, 1)
    sumx(0)
    sumx_in(-3)
    sumy(2, 0)
    sumx_on(-2)
    sumy(4, 2)
    sumx(-1)
    ylast(0)
    ylast(1)
    sumx_in(3)
    sumz(2)
    sumy(4, -1)
    xlast(4)
    ypush(4)
    fwd_main(1)
    sumy(4, 1)
    ystep(3)
    fwd_main(3)
    sumx_in(2)
    sumy(3, 0)
    ylast(-2)
    sumx_on(1)
    sumx_on(0)
    ylast(-3)
    bwd_other(0)
    fwd_main(4)
    ystep(4)
    sumy(5, 2)
    sumx_in(-2)
    sumyx()
    fwd_main(0)
    sumz(3)
    sumx_on(-1)
    bwd_other(2)
    ylast(3)
    sumx_in(1)
    sumy(5, -1)
    bwd_other(1)
    bwd_other(3)
    sumx_in(0)
    ylast(4)
    bwd_send(3)
    bwd_send(2)
    bwd_send(0)
    bwd_send(1)
    sumy(5, 1)
    sumyx_on()
    sumy(4, 0)
    bwd_own(3)
    bwd_rest(3)
    sumx_in(-1)
    fwd_rest(2)
    sumz(4)
    fwd_main(2)
    bwd_out(3)
    sumy(5, 0)
    wout_y()
    fwd_rest(0)
    bwd_own(2)
    bwd_rest(2)
    sumz(5)
    wout_x()
    bwd_out(2)
    bwd_own(0)
    bwd_rest(0)
    fwd_rest(1)
    bwd_out(0)
    bwd_own(1)
    bwd_rest(1)
    bwd_out(1)

    for k in sorted(last):
        last[k].wait_recv()
    for copy in started:
        copy.wait_send()


def body(attn, w, cot):
    vmem = pl.BlockSpec(memory_space=pltpu.VMEM)
    f32s = [
        (NZ, NX, BLK, QUART),
        (4, TOK, ZBLK),
        (4, TOK, ZBLK),
        (4, TOK, ZBLK),
        (NZ, 2, H1, QUART),
        (NZ, 2, S1, QUART),
        (3, 2, S1, QUART),
        (2, H1, QUART),
        (3, 2, NX, S2, QUART),
        (2, NX, H2, QUART),
        (2, H2, QUART),
        (2, S2, QUART),
    ]
    bf16s = [(NY * TOK, 2 * HALF), (NY * TOK, QUART), (NZ, NX, BLK, WIDE), (NZ, NX, BLK, HALF - WIDE), (TOK, HALF)]
    return pl.pallas_call(
        kernel,
        out_shape=(
            jax.ShapeDtypeStruct((TOK, HALF), BF16),
            jax.ShapeDtypeStruct((TOK, HALF), BF16),
            jax.ShapeDtypeStruct((BLK, HALF), F32),
        ),
        in_specs=[vmem] * 3,
        out_specs=(vmem,) * 3,
        scratch_shapes=[pltpu.VMEM(s, BF16) for s in bf16s]
        + [pltpu.VMEM(s, F32) for s in f32s]
        + [pltpu.SemaphoreType.DMA((N_MSG,)), pltpu.SemaphoreType.DMA((N_MSG,))],
        compiler_params=pltpu.CompilerParams(
            collective_id=0, has_side_effects=True, vmem_limit_bytes=56 * 2**20
        ),
        name="projection",
    )(attn, w, cot)


def solution(mesh):
    in_specs = (P(("depth", "row"), "col"), P("row", "col"), P(("depth", "row"), "col"))
    out_specs = (P(("depth", "row"), "col"), P(("depth", "row"), "col"), P("row", "col"))
    return jax.shard_map(body, mesh=mesh, in_specs=in_specs, out_specs=out_specs, check_vma=False)
```

time: 465 us -> 95.8 us (0.21)
  waiting for transfers between devices: 420 us -> 0 us
  Pallas kernels: 0 us -> 90.1 us
  matrix products: 24.7 us -> 0 us
  between operations: 13.8 us -> 0.65 us
    reduce_scatter x2 -> x0, waiting for transfers between devices: 253 us -> none  [the longest x1 243 us: body(): lax.psum_scatter(lax.dot_general(columns, cotangent, (((0,), (0,)), ((),...]
    all_gather x2 -> x0, waiting for transfers between devices: 117 us -> none  [the longest x1 97.9 us: body(): lax.all_gather(w_out, 'row', axis=0, tiled=True)]
    pallas_call x0 -> x1, Pallas kernels: none -> 90.1 us  [body(): pl.pallas_call(kernel, out_shape=(jax.ShapeDtypeStruct((TOK, HALF), BF16)...]
    psum x1 -> x0, waiting for transfers between devices: 48.9 us -> none  [body(): total = lax.psum(row_summed, 'depth')]
    dot_general x3 -> x0, matrix products: 24.7 us -> none  [the longest x1 9.44 us: body(): lax.dot_general(columns, cotangent, (((0,), (0,)), ((), ())), preferred_e...]
  transfers between devices with their start and end apart: 5 -> 0, of which waited for: 5 -> 0; matrix products, arithmetic and copies ran while one was open for 6% -> 0% of each run, Pallas kernels for 0% -> 0%
where the time goes in v2:
time: 95.8 us; the launch traced here: 95.1 us
  Pallas kernels  90.1 us (94%)
  local copies, waits for them, and re-layouts  4.3 us (4%)
    pallas_call x1, Pallas kernels, body(): pl.pallas_call(kernel, out_shape=(jax.ShapeDtypeStruct((TOK, HALF), BF16)...  90.1 us
    unnamed x7, local copies, waits for them, and re-layouts  4.3 us

profile of v2, /device:TPU:16, one launch (start us, length us, event | category | flops | bytes accessed | tf_op | source)
XLA Modules:
  0.0 95.1 jit_solution(5880151031211336953)
XLA Ops:
  0.6 90.1 %projection.1 = (bf16[256,1536]{1,0:T(8,128)(2,1)}, bf16[256,1536]{1,0:T(8,128)(2,1)}, f32[96,1536]{1,0:T(8,128)}) custom-call(bf16[256,1536]{1,0:T(8,128)(2,1)} %attn.1, bf16[96,1536]{1,0:T(8,128)(2,1)} %w.1, bf16[256,1536]{1,0:T(8,128)(2,1)} %cot.1), custom_call_target="tpu_custom_call" | custom-call | tf_op jit(solution)/shard_map/projection/pallas_call | solution.py:526
  90.8 0.0 copy-start
  90.8 2.1 %copy.9 = bf16[256,1536]{1,0:T(8,128)(2,1)} copy(bf16[256,1536]{1,0:T(8,128)(2,1)} %get-tuple-element.6) | data formatting | bytes 1572864
  92.9 0.0 copy-done
  92.9 0.0 copy-start.1
  92.9 0.9 copy.10
  93.8 0.5 copy-done.1
  94.3 0.8 copy.11
Async XLA Ops:
  90.8 2.1 %copy-start = (bf16[256,1536]{1,0:T(8,128)(2,1)S(1)}, bf16[256,1536]{1,0:T(8,128)(2,1)}, u32[]{:S(2)}) copy-start(bf16[256,1536]{1,0:T(8,128)(2,1)} %get-tuple-element.7) | copy-start | bytes 2359300
  92.9 1.3 %copy-start.1 = (f32[96,1536]{1,0:T(8,128)S(1)}, f32[96,1536]{1,0:T(8,128)}, u32[]{:S(2)}) copy-start(f32[96,1536]{1,0:T(8,128)} %get-tuple-element.8) | copy-start | bytes 1769476

commit v3 on v2

--- a/solution.py
+++ b/solution.py
@@ -19,14 +19,13 @@
 S2 = BLK - S1
 H1, H2 = S1 // 2, S2 // 2
 M2 = S1 + H2
-HT = TOK // 2
 ZBLK = NX * BLK
 F32, BF16 = jnp.float32, jnp.bfloat16
-N_MSG = 208
-
-
-def kernel(attn, w, cot, proj, igrad, wgrad, A, CQ, Wp, Wr, cotp, G, bo, bm, br,
-           xa, xb, za, za4, ya, yb, yxa, yxb, send, recv):
+N_MSG = 224
+
+
+def kernel(attn, w, cot, proj, igrad, wgrad, A, CQ, Wp, Wr, Wx, cotp, cotx, pv, iv, G, bo, bm, br,
+           xa, xb, za, za4, ya, yb, yxa, yxb, wv, send, recv, local):
     row, c, y = lax.axis_index("row"), lax.axis_index("col"), lax.axis_index("depth")
     z, x = row // NX, lax.rem(row, NX)
 
@@ -57,22 +56,44 @@
     def same(ref, dev):
         return push(ref, ref, dev)
 
+    moved = []
+
+    def move(src, dst):
+        moved.append(pltpu.make_async_copy(src, dst, local.at[len(moved)]))
+        moved[-1].start()
+
     at, ct, cc, wz, wx, wr, wxr, wy = {}, {}, {}, {}, {}, {}, {}, {}
     gx, gz, gy, gyx, last, back = {}, {}, {}, {}, {}, {}
 
-    def ablk(k, h, r0, n):
-        return A.at[pl.ds(pl.multiple_of(yy(k) * TOK + r0, 128), n), pl.ds(pl.multiple_of(h * HALF, 128), HALF)]
-
-    def att(i):
-        r0 = i * HT
-        at[i, 0] = push(attn.at[pl.ds(r0, HT)], ablk(0, c, r0, HT), yp)
-        r0 = (1 - i) * HT
-        at[i, 1] = push(attn.at[pl.ds(r0, HT)], ablk(0, c, r0, HT), ym)
-
-    def att_on(i):
-        at[0, i].wait_recv()
-        k = -1 if i == 0 else 1
-        at[2, i] = same(ablk(k, c, i * HT, HT), yp if i == 0 else ym)
+    def four(k):
+        return lax.rem(z + k, 4)
+
+    def piece(k, p, h):
+        lane0 = pl.multiple_of(h * HALF + four(k) * ZBLK, 128)
+        return A.at[pl.ds(pl.multiple_of(yy(p) * TOK, TOK), TOK), pl.ds(lane0, ZBLK)]
+
+    def att(k):
+        src = attn.at[:, pl.ds(pl.multiple_of(four(k) * ZBLK, 128), ZBLK)]
+        at[k, 0] = push(src, piece(k, 0, c), yp)
+        at[k, 1] = push(src, piece(k, 0, c), ym)
+
+    def att_on(k):
+        side = 0 if k in (1, 4) else 1
+        at[k, side].wait_recv()
+        at[k, 2] = same(piece(k, 2 * side - 1, c), ym if side else yp)
+
+    def cross(k):
+        at[k, 1 if k in (1, 4) else 0].wait_recv()
+        for p in (-1, 1):
+            cc[k, p] = same(piece(k, p, c), core)
+
+    def cross2(k):
+        at[k, 2].wait_recv()
+        cc[k, 2] = same(piece(k, 2, c), core)
+
+    def cross_in(k):
+        for p in (-1, 1, 2):
+            cc[k, p].wait_recv()
 
     def cots(k):
         q = cot.at[:, pl.ds(pl.multiple_of(yy(k) * QUART, 128), QUART)]
@@ -83,24 +104,20 @@
             ct[k].wait_recv()
 
     def own():
-        cc[0] = push(attn, ablk(0, c, 0, TOK), core)
-        A[pl.ds(pl.multiple_of(y * TOK, TOK), TOK), pl.ds(pl.multiple_of(c * HALF, 128), HALF)] = attn[...]
-        CQ[pl.ds(pl.multiple_of(y * TOK, TOK), TOK), :] = cot[:, pl.ds(pl.multiple_of(y * QUART, 128), QUART)]
-        cotp[:, 0:MAIN] = cot[:, 0:MAIN]
+        at_y = pl.ds(pl.multiple_of(y * TOK, TOK), TOK)
+        mine = A.at[at_y, pl.ds(pl.multiple_of(c * HALF, 128), HALF)]
+        cc[0] = push(attn, mine, core)
+        move(attn, mine)
+        move(cot.at[:, pl.ds(pl.multiple_of(y * QUART, 128), QUART)], CQ.at[at_y, :])
+        move(cot.at[:, pl.ds(0, MAIN)], cotp.at[:, pl.ds(0, MAIN)])
         for j, k in enumerate((0, -1, 1, 2)):
-            lane = pl.multiple_of(MAIN + yy(k) * TILE, TILE)
-            cotp[:, MAIN + j * TILE:MAIN + (j + 1) * TILE] = cot[:, pl.ds(lane, TILE)]
-
-    def cross(k):
-        if k == 2:
-            at[2, 0].wait_recv()
-            at[2, 1].wait_recv()
-        else:
-            at[1, 0 if k == -1 else 1].wait_recv()
-        cc[k] = same(ablk(k, c, 0, TOK), core)
-
-    def cross_in(k):
-        cc[k].wait_recv()
+            move(cot.at[:, pl.ds(lane(k), TILE)], cotp.at[:, pl.ds(MAIN + j * TILE, TILE)])
+
+    def own_in():
+        for copy in moved[2:9]:
+            copy.wait()
+        cc[0].wait_recv()
+        cc[1] = push(cotp.at[:, pl.ds(WIDE, HALF - WIDE)], cotx, core)
 
     def blk(k, r0, n):
         return Wp.at[zz(k), x, pl.ds(r0, n), :]
@@ -184,10 +201,12 @@
         wy[k, 2].wait_recv()
 
     def term(k):
-        zi = zz(k)
-        a = A[:, pl.ds(pl.multiple_of(zi * ZBLK, 128), ZBLK)]
-        g = lax.dot_general(a, CQ[...], (((0,), (0,)), ((), ())), preferred_element_type=F32)
-        G[zi] = g.reshape(NX, BLK, QUART)
+        @pl.loop(0, 2)
+        def _(i):
+            zi = lax.rem(z + k + 4 * i, NZ)
+            a = A[:, pl.ds(pl.multiple_of(zi * ZBLK, 128), ZBLK)]
+            g = lax.dot_general(a, CQ[...], (((0,), (0,)), ((), ())), preferred_element_type=F32)
+            G[zi] = g.reshape(NX, BLK, QUART)
 
     def sumx(k):
         gx[k, 0] = push(G.at[zz(k), xx(2), pl.ds(0, H1)], xa.at[k % NZ, 0], xp)
@@ -259,9 +278,12 @@
 
     def wout(r0, n, g):
         at_y = pl.ds(pl.multiple_of(y * QUART, 128), QUART)
-        wgrad[r0:r0 + n, at_y] = g * (1.0 / math.sqrt(TOK * NZ * NX * NY))
+        wv[r0:r0 + n, :] = g * (1.0 / math.sqrt(TOK * NZ * NX * NY))
+        part = wv.at[pl.ds(r0, n), :]
+        there = wgrad.at[pl.ds(r0, n), at_y]
         for dev in (yp, ym, y2):
-            last[len(last)] = same(wgrad.at[pl.ds(r0, n), at_y], dev)
+            last[len(last)] = push(part, there, dev)
+        move(part, there)
 
     def wout_x():
         wout(0, S1, G[z, x, 0:S1])
@@ -273,241 +295,259 @@
 
     def fwd(src, lo, width, at_col):
         a = A[pl.ds(pl.multiple_of(y * TOK, TOK), TOK), :]
-        p = jnp.dot(a, src[:, :, :, lo:lo + width].reshape(NZ * ZBLK, width), preferred_element_type=F32)
-        proj[:, pl.ds(at_col, width)] = p.astype(BF16)
+        p = jnp.dot(a, src[:, :, :, pl.ds(lo, width)].reshape(NZ * ZBLK, width), preferred_element_type=F32)
+        pv[:, pl.ds(at_col, width)] = p.astype(BF16)
 
     def lane(k):
         return pl.multiple_of(MAIN + yy(k) * TILE, TILE)
 
-    def fwd_main(n):
-        if n < 4:
-            fwd(Wp, 256 * n, 256, 256 * n)
-        else:
-            fwd(Wp, MAIN, TILE, lane(0))
-
-    def fwd_rest(n):
-        fwd(Wr, n * TILE, TILE, lane((-1, 1, 2)[n]))
-
-    def bwd(ref, cols, zi):
-        wide = ref.shape[-1]
-        return lax.dot_general(
-            cols, ref[zi].reshape(ZBLK, wide), (((1,), (1,)), ((), ())), preferred_element_type=F32
-        )
-
-    def bwd_other(j):
-        bo[j] = bwd(Wp, cotp[:, 0:WIDE], 4 * (1 - c) + j)
-
-    def bwd_own(j):
-        bm[j] = bwd(Wp, cotp[:, 0:WIDE], 4 * c + j)
-
-    def bwd_send(j):
-        bo[j] += bwd(Wr, cotp[:, WIDE:], 4 * (1 - c) + j)
-        back[j] = push(bo.at[j], br.at[j], core)
-
-    def bwd_rest(j):
-        bm[j] += bwd(Wr, cotp[:, WIDE:], 4 * c + j)
-
-    def bwd_out(j):
-        back[j].wait_recv()
-        igrad[:, j * ZBLK:(j + 1) * ZBLK] = (bm[j] + br[j]).astype(BF16)
-
-    Wp[z, x, :, 0:MAIN] = w[:, 0:MAIN]
-    Wp[z, x, :, MAIN:WIDE] = w[:, pl.ds(pl.multiple_of(MAIN + TILE * y, TILE), TILE)]
+    def fwd_main():
+        @pl.loop(0, 4)
+        def _(n):
+            lo = pl.multiple_of(n * 256, 256)
+            fwd(Wp, lo, 256, lo)
+
+        fwd(Wp, MAIN, TILE, lane(0))
+        move(pv.at[:, pl.ds(0, MAIN)], proj.at[:, pl.ds(0, MAIN)])
+
+    def fwd_rest():
+        p = jnp.dot(A[pl.ds(pl.multiple_of(y * TOK, TOK), TOK), :], Wr[...].reshape(NZ * ZBLK, HALF - WIDE),
+                    preferred_element_type=F32).astype(BF16)
+        for n, k in enumerate((-1, 1, 2)):
+            pv[:, pl.ds(lane(k), TILE)] = p[:, n * TILE:(n + 1) * TILE]
+        move(pv.at[:, pl.ds(MAIN, HALF - MAIN)], proj.at[:, pl.ds(MAIN, HALF - MAIN)])
+
+    def bwd(cols, panel):
+        panel = panel.reshape(ZBLK, panel.shape[-1])
+        return lax.dot_general(cols, panel, (((1,), (1,)), ((), ())), preferred_element_type=F32)
+
+    def bwd_other():
+        @pl.loop(0, 4)
+        def _(j):
+            bo[j] = bwd(cotp[:, 0:WIDE], Wp[4 * (1 - c) + j])
+
+        back[0] = push(bo, br, core)
+
+    def bwd_own():
+        @pl.loop(0, 4)
+        def _(j):
+            bm[j] = bwd(cotp[:, 0:WIDE], Wp[4 * c + j])
+
+    def bwd_in():
+        back[0].wait_recv()
+        cc[1].wait_recv()
+
+    def wcross(k):
+        back[k] = push(Wr.at[4 * (1 - c) + four(k)], Wx.at[four(k)], core)
+
+    def bwd_out(k):
+        back[k].wait_recv()
+        j = four(k)
+        cols = pl.ds(pl.multiple_of(j * ZBLK, 128), ZBLK)
+        rest = bwd(cotp[:, WIDE:], Wr[4 * c + j]) + bwd(cotx[...], Wx[j])
+        iv[:, cols] = (bm[j] + br[j] + rest).astype(BF16)
+        move(iv.at[:, cols], igrad.at[:, cols])
+
+    move(w.at[:, pl.ds(0, MAIN)], Wp.at[z, x, :, pl.ds(0, MAIN)])
+    move(w.at[:, pl.ds(lane(0), TILE)], Wp.at[z, x, :, pl.ds(MAIN, TILE)])
     barrier = pltpu.get_barrier_semaphore()
     for dev in (zp, zm, xp, xm, yp, ym, y2, core):
         pl.semaphore_signal(barrier, inc=1, device_id=dev, device_id_type=MESH)
     pl.semaphore_wait(barrier, 8)
 
-    att(0)
+    def w_in():
+        for copy in moved[:2]:
+            copy.wait()
+
+    w_in()
+    zpush(1)
+    att(4)
+    own()
     rx()
-    att(1)
-    zpush(1)
+    xpush(0)
     rpush(1, 0)
-    xpush(0)
-    own()
+    att(3)
     rx_on()
     rpush(1, -1)
     rpush(1, 1)
     zstep(1)
+    xpush(1)
+    att(1)
     xpush(-1)
-    xpush(1)
+    own_in()
+    rstep(1, 0)
+    rx_in()
     xstep(0)
-    rstep(1, 0)
-    cross_in(0)
-    rx_in()
+    rstep(1, -1)
+    cots(2)
+    rstep(1, 1)
+    xstep(1)
+    att_on(4)
+    cross(4)
+    att_on(3)
+    cross(3)
     rpush(1, 2)
+    zstep(2)
+    xpush(-2)
+    xstep(-1)
+    xlast(0)
     cots(1)
     cots(-1)
-    rstep(1, -1)
-    rstep(1, 1)
-    xstep(-1)
-    att_on(0)
+    xpush(2)
+    rstep(2, -1)
+    xlast(1)
+    rstep(2, 1)
     att_on(1)
-    zstep(2)
-    xpush(2)
-    xpush(-2)
-    xstep(1)
+    cross(1)
+    rstep(1, 2)
+    xstep(-2)
+    cross2(4)
+    cross2(3)
     rstep(2, 0)
-    xlast(0)
-    rstep(1, 2)
     xlast(-1)
-    rstep(2, -1)
-    cross(-1)
-    cross(1)
-    rstep(2, 1)
-    xstep(2)
-    ypush(-1)
     zstep(3)
     xpush(-3)
-    cots(2)
+    att(2)
     xpush(3)
-    xstep(-2)
+    cross_in(4)
+    rstep(3, -1)
+    cots_in()
+    term(4)
+    cross_in(3)
+    term(3)
+    xlast(-2)
+    rstep(3, 1)
+    sumy(1, 2)
+    rstep(2, 2)
+    sumx(4)
+    ypush(-2)
+    xstep(2)
+    sumy(1, 1)
+    cross2(1)
+    sumy(1, -1)
+    att_on(2)
+    zstep(4)
+    xpush(4)
+    sumy(1, 0)
+    rstep(4, -1)
+    ypush(1)
     rstep(3, 0)
-    cross_in(-1)
-    xlast(1)
-    ypush(1)
-    rstep(2, 2)
+    rstep(4, 1)
+    cross_in(1)
+    term(1)
+    sumy(2, 2)
+    ypush(-1)
+    cross(2)
+    xstep(3)
+    rstep(3, 2)
+    sumy(2, 1)
+    sumx_on(4)
     xlast(2)
     ypush(2)
-    rstep(3, -1)
-    cross_in(1)
-    rstep(3, 1)
+    sumy(2, -1)
+    cross2(2)
+    sumx(-3)
+    ystep(-2)
+    rstep(4, 0)
+    xstep(-3)
+    sumy(2, 0)
+    ystep(1)
+    sumx(3)
+    cross_in(2)
+    term(2)
+    xlast(3)
+    sumx(-2)
+    ypush(3)
+    xstep(4)
+    sumy(3, 2)
+    rstep(4, 2)
+    sumy(3, 1)
+    sumx_in(4)
+    ystep(-1)
+    ystep(2)
+    sumx(2)
+    sumz(1)
+    sumx_on(-3)
+    sumy(3, -1)
     ypush(0)
-    xstep(-3)
-    zstep(4)
-    xpush(4)
-    cross(2)
-    rstep(4, 0)
-    xstep(3)
-    rstep(3, 2)
-    ystep(-1)
-    rstep(4, -1)
-    xlast(-2)
-    ypush(-2)
-    rstep(4, 1)
-    rstep(4, 2)
-    cots_in()
     xlast(-3)
+    ylast(-2)
+    sumx(1)
+    sumy(3, 0)
+    ylast(1)
+    sumx_on(3)
     ypush(-3)
-    cross_in(2)
-    term(4)
-    sumy(1, 2)
-    sumy(1, -1)
-    sumy(1, 0)
-    sumx(4)
-    ystep(1)
-    term(-3)
-    sumy(1, 1)
-    ystep(2)
-    term(3)
-    xlast(3)
-    sumx(3)
-    sumy(2, 2)
-    sumx(-3)
-    term(-2)
+    sumy(4, 2)
+    sumx_on(-2)
+    xlast(4)
+    bwd_other()
+    ylast(2)
+    ystep(3)
+    sumy(4, 1)
+    sumx(-1)
+    ylast(-1)
+    sumx_on(2)
+    sumx_in(-3)
+    fwd_main()
     ystep(0)
-    sumx_on(4)
-    sumx(-2)
-    sumy(2, -1)
-    sumy(2, 1)
-    term(2)
-    sumx(2)
-    ystep(-2)
-    ylast(-1)
-    sumx_on(-3)
-    sumy(3, 2)
-    sumx_on(3)
-    xstep(4)
-    term(1)
-    sumx_in(4)
-    sumz(1)
-    sumy(3, -1)
-    term(-1)
-    ypush(3)
-    sumx(1)
-    sumx_on(2)
-    term(0)
-    ystep(-3)
-    ylast(2)
-    sumy(3, 1)
-    sumx(0)
-    sumx_in(-3)
-    sumy(2, 0)
-    sumx_on(-2)
-    sumy(4, 2)
-    sumx(-1)
-    ylast(0)
-    ylast(1)
     sumx_in(3)
     sumz(2)
     sumy(4, -1)
-    xlast(4)
     ypush(4)
-    fwd_main(1)
-    sumy(4, 1)
-    ystep(3)
-    fwd_main(3)
-    sumx_in(2)
-    sumy(3, 0)
-    ylast(-2)
-    sumx_on(1)
-    sumx_on(0)
-    ylast(-3)
-    bwd_other(0)
-    fwd_main(4)
-    ystep(4)
+    ystep(-3)
     sumy(5, 2)
     sumx_in(-2)
     sumyx()
-    fwd_main(0)
+    sumy(4, 0)
+    sumx_on(1)
+    sumx(0)
+    sumx_on(-1)
+    sumy(5, 1)
+    wcross(2)
+    bwd_own()
+    sumx_in(2)
     sumz(3)
-    sumx_on(-1)
-    bwd_other(2)
+    ylast(0)
     ylast(3)
+    wcross(3)
+    sumy(5, -1)
+    sumyx_on()
     sumx_in(1)
-    sumy(5, -1)
-    bwd_other(1)
-    bwd_other(3)
+    ystep(4)
+    bwd_in()
+    sumx_on(0)
+    sumy(5, 0)
+    ylast(-3)
+    wcross(1)
+    bwd_out(2)
+    sumx_in(-1)
+    sumz(4)
+    bwd_out(3)
+    wout_y()
+    ylast(4)
+    wcross(4)
+    fwd_rest()
+    bwd_out(1)
     sumx_in(0)
-    ylast(4)
-    bwd_send(3)
-    bwd_send(2)
-    bwd_send(0)
-    bwd_send(1)
-    sumy(5, 1)
-    sumyx_on()
-    sumy(4, 0)
-    bwd_own(3)
-    bwd_rest(3)
-    sumx_in(-1)
-    fwd_rest(2)
-    sumz(4)
-    fwd_main(2)
-    bwd_out(3)
-    sumy(5, 0)
-    wout_y()
-    fwd_rest(0)
-    bwd_own(2)
-    bwd_rest(2)
     sumz(5)
     wout_x()
-    bwd_out(2)
-    bwd_own(0)
-    bwd_rest(0)
-    fwd_rest(1)
-    bwd_out(0)
-    bwd_own(1)
-    bwd_rest(1)
-    bwd_out(1)
+    bwd_out(4)
 
     for k in sorted(last):
         last[k].wait_recv()
     for copy in started:
         copy.wait_send()
+    for copy in moved[9:]:
+        copy.wait()
+
+
+def pass_on(*refs):
+    for i in range(3):
+        refs[i + 3][...] = refs[i][...]
 
 
 def body(attn, w, cot):
-    vmem = pl.BlockSpec(memory_space=pltpu.VMEM)
+    whole = pl.BlockSpec(memory_space=pl.ANY)
     f32s = [
         (NZ, NX, BLK, QUART),
         (4, TOK, ZBLK),
@@ -521,25 +561,27 @@
         (2, NX, H2, QUART),
         (2, H2, QUART),
         (2, S2, QUART),
+        (BLK, QUART),
     ]
-    bf16s = [(NY * TOK, 2 * HALF), (NY * TOK, QUART), (NZ, NX, BLK, WIDE), (NZ, NX, BLK, HALF - WIDE), (TOK, HALF)]
-    return pl.pallas_call(
+    rest = HALF - WIDE
+    bf16s = [(NY * TOK, 2 * HALF), (NY * TOK, QUART), (NZ, NX, BLK, WIDE), (NZ, NX, BLK, rest), (4, NX, BLK, rest)]
+    bf16s += [(TOK, HALF), (TOK, rest), (TOK, HALF), (TOK, HALF)]
+    outs = tuple(pltpu.VMEM((n, HALF), t) for n, t in ((TOK, BF16), (TOK, BF16), (BLK, F32)))
+    attn, w, cot = (pltpu.with_memory_space_constraint(v, pltpu.HBM) for v in (attn, w, cot))
+    done = pl.pallas_call(
         kernel,
-        out_shape=(
-            jax.ShapeDtypeStruct((TOK, HALF), BF16),
-            jax.ShapeDtypeStruct((TOK, HALF), BF16),
-            jax.ShapeDtypeStruct((BLK, HALF), F32),
-        ),
-        in_specs=[vmem] * 3,
-        out_specs=(vmem,) * 3,
+        out_shape=outs,
+        in_specs=[whole] * 3,
+        out_specs=(whole,) * 3,
         scratch_shapes=[pltpu.VMEM(s, BF16) for s in bf16s]
         + [pltpu.VMEM(s, F32) for s in f32s]
-        + [pltpu.SemaphoreType.DMA((N_MSG,)), pltpu.SemaphoreType.DMA((N_MSG,))],
+        + [pltpu.SemaphoreType.DMA((N_MSG,)), pltpu.SemaphoreType.DMA((N_MSG,)), pltpu.SemaphoreType.DMA((20,))],
         compiler_params=pltpu.CompilerParams(
-            collective_id=0, has_side_effects=True, vmem_limit_bytes=56 * 2**20
+            collective_id=0, has_side_effects=True, vmem_limit_bytes=40 * 2**20
         ),
         name="projection",
     )(attn, w, cot)
+    return done
 
 
 def solution(mesh):

time: 95.8 us -> 90 us (0.939)
  Pallas kernels: 90.1 us -> 86.7 us
  local copies, waits for them, and re-layouts: 4.3 us -> 2.58 us
    pallas_call x1, Pallas kernels: 90.1 us -> 86.7 us  [body(): pl.pallas_call(kernel, out_shape=outs, in_specs=[whole] * 3, out_specs=(w...]
    unnamed x7 -> x3, local copies, waits for them, and re-layouts: 4.3 us -> 2.58 us
where the time goes in v3:
time: 90 us; the launch traced here: 89.9 us
  Pallas kernels  86.7 us (96%)
  local copies, waits for them, and re-layouts  2.58 us (3%)
    pallas_call x1, Pallas kernels, body(): pl.pallas_call(kernel, out_shape=outs, in_specs=[whole] * 3, out_specs=(w...  86.7 us
    unnamed x3, local copies, waits for them, and re-layouts  2.58 us

profile of v3, /device:TPU:16, one launch (start us, length us, event | category | flops | bytes accessed | tf_op | source)
XLA Modules:
  0.0 89.9 jit_solution(4495443202739960346)
XLA Ops:
  0.6 86.7 %projection.1 = (bf16[256,1536]{1,0:T(8,128)(2,1)S(1)}, bf16[256,1536]{1,0:T(8,128)(2,1)S(1)}, f32[96,1536]{1,0:T(8,128)S(1)}) custom-call(bf16[256,1536]{1,0:T(8,128)(2,1)} %attn.1, bf16[96,1536]{1,0:T(8,128)(2,1)} %w.1, bf16[256,1536]{1,0:T(8,128)(2,1)} %cot.1), custom_call_target="tpu_custom_call" | custom-call | tf_op jit(solution)/shard_map/projection/pallas_call | solution.py:571
  87.4 0.9 copy.9
  88.2 0.8 copy.11
  89.1 0.9 copy.10

commit v4 on v3

v4 whole, which is shorter than its diff:
```python
import math

import jax
import jax.numpy as jnp
from jax import lax
from jax.experimental import pallas as pl
from jax.experimental.pallas import tpu as pltpu
from jax.sharding import PartitionSpec as P

MESH = pl.DeviceIdType.MESH
NZ, NX, NY = 8, 4, 4
TOK, HALF, BLK = 256, 1536, 96
MAIN, TILE = 1024, 128
WIDE = MAIN + TILE
ROWS, COLS = BLK // 2, HALF // 2
R1 = 64
R2 = BLK - R1
S1 = ROWS // 2
C1 = COLS // 2
ZBLK = NX * BLK
PIECE = 2 * NX * ROWS
F32, BF16 = jnp.float32, jnp.bfloat16
N_MSG = 224


def kernel(attn, w, cot, proj, igrad, wgrad, A, AH, AO, CQ, PM, Wp, Wr, Wx, cotp, cotx, pv, iv, G, bo, bm, br,
           xa, xb, za, za4, ya, yb, yxa, yxb, wv, send, recv, local):
    row, c, y = lax.axis_index("row"), lax.axis_index("col"), lax.axis_index("depth")
    z, x = row // NX, lax.rem(row, NX)

    def zz(k):
        return lax.rem(z + (k % NZ), NZ)

    def xx(k):
        return lax.rem(x + (k % NX), NX)

    def yy(k):
        return lax.rem(y + k, NY)

    zp, zm = (zz(1) * NX + x, c, y), (zz(-1) * NX + x, c, y)
    xp, xm = (z * NX + xx(1), c, y), (z * NX + xx(-1), c, y)
    yh, yd = yy(1 - 2 * lax.rem(y, 2)), yy(3 + 2 * lax.rem(y, 2))
    my_h, my_d = y // 2, lax.rem((y + 1) // 2, 2)
    ph, pd, y2 = (row, c, yh), (row, c, yd), (row, c, yy(2))
    core = (row, 1 - c, y)
    started = []

    def push(src, dst, dev):
        k = len(started)
        copy = pltpu.make_async_remote_copy(
            src_ref=src, dst_ref=dst, send_sem=send.at[k], recv_sem=recv.at[k], device_id=dev, device_id_type=MESH
        )
        copy.start()
        started.append(copy)
        return copy

    def same(ref, dev):
        return push(ref, ref, dev)

    moved = []

    def move(src, dst):
        moved.append(pltpu.make_async_copy(src, dst, local.at[len(moved)]))
        moved[-1].start()

    at, ct, cc, wz, wx, wr, wxr, wy = {}, {}, {}, {}, {}, {}, {}, {}
    gx, gz, gy, gyx, last, back = {}, {}, {}, {}, {}, {}

    def four(k):
        return lax.rem(z + k, 4)

    def own():
        move(attn, A.at[:, pl.ds(pl.multiple_of(c * HALF, 128), HALF)])
        at_y = pl.ds(pl.multiple_of(y * TOK, TOK), TOK)
        move(cot.at[:, pl.ds(pl.multiple_of(my_d * COLS, 128), COLS)], CQ.at[at_y, :])
        move(cot.at[:, pl.ds(0, MAIN)], cotp.at[:, pl.ds(0, MAIN)])
        for j, k in enumerate((y, yh, yd, yy(2))):
            move(cot.at[:, pl.ds(lane(k), TILE)], cotp.at[:, pl.ds(MAIN + j * TILE, TILE)])

    def own_push():
        cc[0] = push(attn, A.at[:, pl.ds(pl.multiple_of(c * HALF, 128), HALF)], core)

    def own_in():
        for copy in moved[3:9]:
            copy.wait()
        cc[0].wait_recv()
        cc[1] = push(cotp.at[:, pl.ds(WIDE, HALF - WIDE)], cotx, core)

    def piece(p, who, side):
        lane0 = pl.multiple_of(side * COLS + (p - 1) * PIECE, 128)
        return AH.at[pl.ds(pl.multiple_of(who * TOK, TOK), TOK), pl.ds(lane0, PIECE)]

    def perm(p):
        if p == 1:
            moved[2].wait()
            src = lax.broadcasted_iota(jnp.int32, (ZBLK, PIECE), 0)
            dst = lax.broadcasted_iota(jnp.int32, (ZBLK, PIECE), 1)
            for second in (0, 1):
                d = dst - second * (PIECE // 2)
                ok = (d >= 0) & (d < PIECE // 2)
                for n in range(1, NX):
                    d = d + jnp.where(dst >= second * (PIECE // 2) + n * ROWS, BLK - ROWS, 0)
                for other in (0, 1):
                    half = my_h + other - 2 * my_h * other
                    PM[second, other] = jnp.where(ok & (src == d + ROWS * half), 1.0, 0.0).astype(BF16)
        ks = (4, 3) if p == 1 else (1, 2)
        cols = [A[:, pl.ds(pl.multiple_of(c * HALF + four(k) * ZBLK, 128), ZBLK)] for k in ks]
        for other in (0, 1):
            g = sum(jnp.dot(cols[n], PM[n, other], preferred_element_type=F32) for n in (0, 1)).astype(BF16)
            if other:
                AO[p - 1] = g
            else:
                lane0 = pl.multiple_of(c * COLS + (p - 1) * PIECE, 128)
                AH[pl.ds(pl.multiple_of(y * TOK, TOK), TOK), pl.ds(lane0, PIECE)] = g

    def att(p):
        at[p, 0] = same(piece(p, y, c), ph)
        at[p, 1] = push(AO.at[p - 1], piece(p, y, c), pd)
        cc[p, 0] = same(piece(p, y, c), core)

    def att_on(p):
        at[p, 1].wait_recv()
        at[p, 2] = same(piece(p, yd, c), ph)
        cc[p, 1] = same(piece(p, yd, c), core)

    def cross(p):
        at[p, 0].wait_recv()
        cc[p, 2] = same(piece(p, yh, c), core)

    def cross2(p):
        at[p, 2].wait_recv()
        cc[p, 3] = same(piece(p, yy(2), c), core)

    def cross_in(p):
        for i in range(4):
            cc[p, i].wait_recv()

    def crow(who):
        return CQ.at[pl.ds(pl.multiple_of(who * TOK, TOK), TOK), :]

    def cots():
        ct[0] = push(cot.at[:, pl.ds(pl.multiple_of((1 - my_d) * COLS, 128), COLS)], crow(y), ph)
        ct[1] = push(cot.at[:, pl.ds(pl.multiple_of(my_d * COLS, 128), COLS)], crow(y), pd)

    def cots_on():
        ct[0].wait_recv()
        ct[2] = same(crow(yh), pd)

    def cots_in():
        ct[1].wait_recv()
        ct[2].wait_recv()

    def blk(k, r0, n):
        return Wp.at[zz(k), x, pl.ds(r0, n), :]

    def zpush(step):
        k, h = step - 1, R1 // 2
        if step < 4:
            wz[step, 0] = same(blk(-k, 0, R1), zp)
            wz[step, 1] = same(blk(k, 0, R1), zm)
        else:
            wz[step, 0] = same(blk(-k, 0, h), zp)
            wz[step, 1] = same(blk(k, h, h), zm)

    def zstep(step):
        wz[step, 0].wait_recv()
        wz[step, 1].wait_recv()
        if step < 4:
            zpush(step + 1)

    def xpush(k):
        wx[k, 0] = same(blk(k, 0, R1), xp)
        wx[k, 1] = same(blk(k, 0, R1), xm)

    def xstep(k):
        h = R1 // 2
        wx[k, 0].wait_recv()
        wx[k, 2] = same(Wp.at[zz(k), xx(-1), pl.ds(0, h), :], xp)
        wx[k, 1].wait_recv()
        wx[k, 3] = same(Wp.at[zz(k), xx(1), pl.ds(h, h), :], xm)

    def xlast(k):
        wx[k, 2].wait_recv()
        wx[k, 3].wait_recv()

    def rx():
        mine = Wp.at[z, x, pl.ds(R1, R2), :]
        wxr[0] = same(mine, xp)
        wxr[1] = same(mine, xm)

    def rx_on():
        h = R2 // 2
        wxr[0].wait_recv()
        wxr[2] = same(Wp.at[z, xx(-1), pl.ds(R1, h), :], xp)
        wxr[1].wait_recv()
        wxr[3] = same(Wp.at[z, xx(1), pl.ds(R1 + h, h), :], xm)

    def rx_in():
        wxr[2].wait_recv()
        wxr[3].wait_recv()

    def rpush(step, j):
        k, h = step - 1, R2 // 2
        if step < 4:
            wr[step, j, 0] = same(Wp.at[zz(-k), xx(j), pl.ds(R1, R2), :], zp)
            wr[step, j, 1] = same(Wp.at[zz(k), xx(j), pl.ds(R1, R2), :], zm)
        else:
            wr[step, j, 0] = same(Wp.at[zz(-k), xx(j), pl.ds(R1, h), :], zp)
            wr[step, j, 1] = same(Wp.at[zz(k), xx(j), pl.ds(R1 + h, h), :], zm)

    def rstep(step, j):
        wr[step, j, 0].wait_recv()
        wr[step, j, 1].wait_recv()
        if step < 4:
            rpush(step + 1, j)

    def wtile(k, j):
        return Wr.at[zz(k), :, :, pl.ds(j * TILE, TILE)]

    def ypush(k):
        src = Wp.at[zz(k), :, :, pl.ds(MAIN, TILE)]
        wy[k, 0] = push(src, wtile(k, 0), ph)
        wy[k, 1] = push(src, wtile(k, 1), pd)

    def ystep(k):
        j = k % 2
        wy[k, j].wait_recv()
        wy[k, 2] = push(wtile(k, j), wtile(k, 2), ph if j else pd)

    def ylast(k):
        wy[k, 1 - k % 2].wait_recv()
        wy[k, 2].wait_recv()

    def term(p):
        ka, kb = (4, 3) if p == 1 else (1, 2)

        @pl.loop(0, 2)
        def _(i):
            a = AH[:, pl.ds(pl.multiple_of(i * COLS + (p - 1) * PIECE, 128), PIECE)]
            g = lax.dot_general(a, CQ[...], (((0,), (0,)), ((), ())), preferred_element_type=F32)
            g = g.reshape(2, NX, ROWS, COLS)
            G[4 * i + four(ka)] = g[0]
            G[4 * i + four(kb)] = g[1]

    lo, hi = pl.ds(0, C1), pl.ds(C1, C1)
    ra, rb = pl.ds(0, S1), pl.ds(S1, S1)

    def sumx(k):
        gx[k, 0] = push(G.at[zz(k), xx(2), ra, lo], xa.at[k % NZ, 0], xp)
        gx[k, 1] = push(G.at[zz(k), xx(2), ra, hi], xa.at[k % NZ, 1], xm)

    def sumx_on(k):
        gx[k, 0].wait_recv()
        G[zz(k), xx(1), 0:S1, 0:C1] += xa[k % NZ, 0]
        gx[k, 2] = push(G.at[zz(k), xx(1), ra], xb.at[k % NZ, 0], xp)
        gx[k, 1].wait_recv()
        G[zz(k), xx(-1), 0:S1, C1:] += xa[k % NZ, 1]
        gx[k, 3] = push(G.at[zz(k), xx(-1), ra], xb.at[k % NZ, 1], xm)

    def sumx_in(k):
        gx[k, 2].wait_recv()
        gx[k, 3].wait_recv()
        G[zz(k), x, 0:S1] += xb[k % NZ, 0] + xb[k % NZ, 1]

    def sumz(step):
        if step == 1:
            gz[1, 0] = push(G.at[zz(4), x, ra, lo], za4.at[0], zp)
            gz[1, 1] = push(G.at[zz(4), x, ra, hi], za4.at[1], zm)
            return
        gz[step - 1, 0].wait_recv()
        gz[step - 1, 1].wait_recv()
        if step == 2:
            G[zz(3), x, 0:S1, 0:C1] += za4[0]
            G[zz(-3), x, 0:S1, C1:] += za4[1]
        elif step < 5:
            G[zz(5 - step), x, 0:S1] += za[step - 3, 0]
            G[zz(step - 5), x, 0:S1] += za[step - 3, 1]
        else:
            G[z, x, 0:S1] += za[2, 0] + za[2, 1]
            return
        gz[step, 0] = push(G.at[zz(5 - step), x, ra], za.at[step - 2, 0], zp)
        gz[step, 1] = push(G.at[zz(step - 5), x, ra], za.at[step - 2, 1], zm)

    def sumy(step, j):
        i, d = xx(j), j % NX
        if step == 1:
            gy[1, j, 0] = push(G.at[zz(4), i, rb, lo], yb.at[0, d], zp)
            gy[1, j, 1] = push(G.at[zz(4), i, rb, hi], yb.at[1, d], zm)
            return
        gy[step - 1, j, 0].wait_recv()
        gy[step - 1, j, 1].wait_recv()
        if step == 2:
            G[zz(3), i, S1:, 0:C1] += yb[0, d]
            G[zz(-3), i, S1:, C1:] += yb[1, d]
        elif step < 5:
            G[zz(5 - step), i, S1:] += ya[step - 3, 0, d]
            G[zz(step - 5), i, S1:] += ya[step - 3, 1, d]
        else:
            G[z, i, S1:] += ya[2, 0, d] + ya[2, 1, d]
            return
        gy[step, j, 0] = push(G.at[zz(5 - step), i, rb], ya.at[step - 2, 0, d], zp)
        gy[step, j, 1] = push(G.at[zz(step - 5), i, rb], ya.at[step - 2, 1, d], zm)

    def sumyx():
        gyx[0] = push(G.at[z, xx(2), rb, lo], yxa.at[0], xp)
        gyx[1] = push(G.at[z, xx(2), rb, hi], yxa.at[1], xm)

    def sumyx_on():
        gyx[0].wait_recv()
        G[z, xx(1), S1:, 0:C1] += yxa[0]
        gyx[2] = push(G.at[z, xx(1), rb], yxb.at[0], xp)
        gyx[1].wait_recv()
        G[z, xx(-1), S1:, C1:] += yxa[1]
        gyx[3] = push(G.at[z, xx(-1), rb], yxb.at[1], xm)

    def wout(r0, g):
        wv[r0:r0 + S1, :] = g * (1.0 / math.sqrt(TOK * NZ * NX * NY))
        part = wv.at[pl.ds(r0, S1), :]
        there = wgrad.at[pl.ds(pl.multiple_of(my_h * ROWS + r0, 8), S1), pl.ds(pl.multiple_of(my_d * COLS, 128), COLS)]
        for dev in (ph, pd, y2):
            last[len(last)] = push(part, there, dev)
        move(part, there)

    def wout_x():
        wout(0, G[z, x, 0:S1])

    def wout_y():
        gyx[2].wait_recv()
        gyx[3].wait_recv()
        wout(S1, G[z, x, S1:] + (yxb[0] + yxb[1]))

    def fwd(src, lane0, width, at_col):
        p = jnp.dot(A[...], src[:, :, :, pl.ds(lane0, width)].reshape(NZ * ZBLK, width), preferred_element_type=F32)
        pv[:, pl.ds(at_col, width)] = p.astype(BF16)

    def lane(who):
        return pl.multiple_of(MAIN + who * TILE, TILE)

    def fwd_main():
        @pl.loop(0, 4)
        def _(n):
            lane0 = pl.multiple_of(n * 256, 256)
            fwd(Wp, lane0, 256, lane0)

        fwd(Wp, MAIN, TILE, lane(y))
        move(pv.at[:, pl.ds(0, MAIN)], proj.at[:, pl.ds(0, MAIN)])

    def fwd_rest():
        p = jnp.dot(A[...], Wr[...].reshape(NZ * ZBLK, HALF - WIDE),
                    preferred_element_type=F32).astype(BF16)
        for n, k in enumerate((yh, yd, yy(2))):
            pv[:, pl.ds(lane(k), TILE)] = p[:, n * TILE:(n + 1) * TILE]
        move(pv.at[:, pl.ds(MAIN, HALF - MAIN)], proj.at[:, pl.ds(MAIN, HALF - MAIN)])

    def bwd(cols, panel):
        panel = panel.reshape(ZBLK, panel.shape[-1])
        return lax.dot_general(cols, panel, (((1,), (1,)), ((), ())), preferred_element_type=F32)

    def bwd_other():
        @pl.loop(0, 4)
        def _(j):
            bo[j] = bwd(cotp[:, 0:WIDE], Wp[4 * (1 - c) + j])

        back[0] = push(bo, br, core)

    def bwd_own():
        @pl.loop(0, 4)
        def _(j):
            bm[j] = bwd(cotp[:, 0:WIDE], Wp[4 * c + j])

    def bwd_in():
        back[0].wait_recv()
        cc[1].wait_recv()

    def wcross(k):
        back[k] = push(Wr.at[4 * (1 - c) + four(k)], Wx.at[four(k)], core)

    def bwd_out(k):
        back[k].wait_recv()
        j = four(k)
        cols = pl.ds(pl.multiple_of(j * ZBLK, 128), ZBLK)
        rest = bwd(cotp[:, WIDE:], Wr[4 * c + j]) + bwd(cotx[...], Wx[j])
        iv[:, cols] = (bm[j] + br[j] + rest).astype(BF16)
        move(iv.at[:, cols], igrad.at[:, cols])

    move(w.at[:, pl.ds(0, MAIN)], Wp.at[z, x, :, pl.ds(0, MAIN)])
    move(w.at[:, pl.ds(lane(y), TILE)], Wp.at[z, x, :, pl.ds(MAIN, TILE)])
    barrier = pltpu.get_barrier_semaphore()
    for dev in (zp, zm, xp, xm, ph, pd, y2, core):
        pl.semaphore_signal(barrier, inc=1, device_id=dev, device_id_type=MESH)
    pl.semaphore_wait(barrier, 8)

    def w_in():
        for copy in moved[:2]:
            copy.wait()

    cots()
    w_in()
    rx()
    zpush(1)
    xpush(0)
    rpush(1, 0)
    own()
    own_push()
    perm(1)
    perm(2)
    rx_on()
    rpush(1, 1)
    rpush(1, -1)
    own_in()
    att(1)
    zstep(1)
    xpush(-1)
    xpush(1)
    rx_in()
    rpush(1, 2)
    xstep(0)
    att(2)
    rstep(1, -1)
    xstep(-1)
    rstep(1, 1)
    cots_on()
    zstep(2)
    xstep(1)
    att_on(1)
    cross(1)
    xpush(-2)
    xlast(0)
    rstep(1, 2)
    xlast(-1)
    xpush(2)
    cross(2)
    att_on(2)
    rstep(2, 1)
    xlast(1)
    rstep(1, 0)
    zstep(3)
    ypush(-1)
    xstep(-2)
    xpush(-3)
    cross2(1)
    rstep(2, 2)
    ypush(0)
    cross_in(1)
    rstep(3, 1)
    xstep(2)
    rstep(2, -1)
    ypush(1)
    cots_in()
    term(1)
    sumy(1, 2)
    sumy(1, 1)
    sumx(4)
    ystep(-1)
    cross2(2)
    xpush(3)
    sumy(1, -1)
    zstep(4)
    xlast(-2)
    rstep(3, 2)
    rstep(4, 1)
    ystep(0)
    xpush(4)
    rstep(2, 0)
    ypush(-2)
    cross_in(2)
    xlast(2)
    term(2)
    ypush(2)
    sumy(2, 2)
    xstep(-3)
    sumy(2, 1)
    ystep(1)
    ylast(0)
    ylast(-1)
    rstep(4, 2)
    xstep(3)
    rstep(3, -1)
    sumy(2, -1)
    ystep(-2)
    sumx_on(4)
    rstep(3, 0)
    xstep(4)
    ystep(2)
    sumy(3, 2)
    xlast(-3)
    ypush(-3)
    sumx(-1)
    sumy(3, 1)
    ylast(-2)
    rstep(4, -1)
    ylast(1)
    sumx(3)
    xlast(3)
    ypush(3)
    sumx(-2)
    sumy(1, 0)
    sumx(-3)
    sumy(3, -1)
    sumx_in(4)
    ylast(2)
    wcross(2)
    rstep(4, 0)
    sumx(1)
    sumx(2)
    sumz(1)
    xlast(4)
    ypush(4)
    fwd_main()
    sumy(4, 2)
    sumx_on(3)
    ystep(3)
    sumy(4, 1)
    sumx_on(-3)
    sumy(2, 0)
    sumx_on(-2)
    ystep(-3)
    bwd_own()
    sumx_on(2)
    sumy(4, -1)
    ystep(4)
    bwd_other()
    sumx_in(3)
    sumy(5, 2)
    sumyx()
    sumx_in(-3)
    sumz(2)
    sumy(5, 1)
    sumx(0)
    sumx_on(1)
    ylast(3)
    wcross(3)
    ylast(-3)
    wcross(1)
    sumx_in(-2)
    sumy(3, 0)
    ylast(4)
    wcross(4)
    fwd_rest()
    sumx_on(-1)
    sumy(5, -1)
    sumx_in(2)
    sumyx_on()
    sumz(3)
    bwd_in()
    bwd_out(2)
    sumx_on(0)
    bwd_out(3)
    sumy(4, 0)
    sumx_in(1)
    bwd_out(1)
    bwd_out(4)
    sumx_in(-1)
    sumz(4)
    sumy(5, 0)
    wout_y()
    sumx_in(0)
    sumz(5)
    wout_x()

    for k in sorted(last):
        last[k].wait_recv()
    for copy in started:
        copy.wait_send()
    for copy in moved[9:]:
        copy.wait()


def pass_on(*refs):
    for i in range(3):
        refs[i + 3][...] = refs[i][...]


def body(attn, w, cot):
    whole = pl.BlockSpec(memory_space=pl.ANY)
    f32s = [
        (NZ, NX, ROWS, COLS),
        (4, TOK, ZBLK),
        (4, TOK, ZBLK),
        (4, TOK, ZBLK),
        (NZ, 2, S1, C1),
        (NZ, 2, S1, COLS),
        (3, 2, S1, COLS),
        (2, S1, C1),
        (3, 2, NX, S1, COLS),
        (2, NX, S1, C1),
        (2, S1, C1),
        (2, S1, COLS),
        (ROWS, COLS),
    ]
    rest = HALF - WIDE
    bf16s = [(TOK, 2 * HALF), (NY * TOK, HALF), (2, TOK, PIECE), (NY * TOK, COLS), (2, 2, ZBLK, PIECE)]
    bf16s += [(NZ, NX, BLK, WIDE), (NZ, NX, BLK, rest), (4, NX, BLK, rest)]
    bf16s += [(TOK, HALF), (TOK, rest), (TOK, HALF), (TOK, HALF)]
    outs = tuple(pltpu.VMEM((n, HALF), t) for n, t in ((TOK, BF16), (TOK, BF16), (BLK, F32)))
    attn, w, cot = (pltpu.with_memory_space_constraint(v, pltpu.HBM) for v in (attn, w, cot))
    done = pl.pallas_call(
        kernel,
        out_shape=outs,
        in_specs=[whole] * 3,
        out_specs=(whole,) * 3,
        scratch_shapes=[pltpu.VMEM(s, BF16) for s in bf16s]
        + [pltpu.VMEM(s, F32) for s in f32s]
        + [pltpu.SemaphoreType.DMA((N_MSG,)), pltpu.SemaphoreType.DMA((N_MSG,)), pltpu.SemaphoreType.DMA((20,))],
        compiler_params=pltpu.CompilerParams(
            collective_id=0, has_side_effects=True, vmem_limit_bytes=40 * 2**20
        ),
        name="projection",
    )(attn, w, cot)
    return done


def solution(mesh):
    in_specs = (P(("depth", "row"), "col"), P("row", "col"), P(("depth", "row"), "col"))
    out_specs = (P(("depth", "row"), "col"), P(("depth", "row"), "col"), P("row", "col"))
    return jax.shard_map(body, mesh=mesh, in_specs=in_specs, out_specs=out_specs, check_vma=False)
```

time: 90 us -> 87.7 us (0.974)
  Pallas kernels: 86.7 us -> 83.7 us
    pallas_call x1, Pallas kernels: 86.7 us -> 83.7 us  [body(): pl.pallas_call(kernel, out_shape=outs, in_specs=[whole] * 3, out_specs=(w...]
where the time goes in v4:
time: 87.7 us; the launch traced here: 86.9 us
  Pallas kernels  83.7 us (95%)
  local copies, waits for them, and re-layouts  2.58 us (3%)
    pallas_call x1, Pallas kernels, body(): pl.pallas_call(kernel, out_shape=outs, in_specs=[whole] * 3, out_specs=(w...  83.7 us
    unnamed x3, local copies, waits for them, and re-layouts  2.58 us

profile of v4, /device:TPU:16, one launch (start us, length us, event | category | flops | bytes accessed | tf_op | source)
XLA Modules:
  0.0 86.9 jit_solution(4750109972918012524)
XLA Ops:
  0.6 83.7 %projection.1 = (bf16[256,1536]{1,0:T(8,128)(2,1)S(1)}, bf16[256,1536]{1,0:T(8,128)(2,1)S(1)}, f32[96,1536]{1,0:T(8,128)S(1)}) custom-call(bf16[256,1536]{1,0:T(8,128)(2,1)} %attn.1, bf16[96,1536]{1,0:T(8,128)(2,1)} %w.1, bf16[256,1536]{1,0:T(8,128)(2,1)} %cot.1), custom_call_target="tpu_custom_call" | custom-call | tf_op jit(solution)/shard_map/projection/pallas_call | solution.py:597
  84.3 0.9 %copy.9 = bf16[256,1536]{1,0:T(8,128)(2,1)} copy(bf16[256,1536]{1,0:T(8,128)(2,1)S(1)} %get-tuple-element.3) | data formatting | bytes 1572864
  85.2 0.8 copy.11
  86.0 0.9 %copy.10 = bf16[256,1536]{1,0:T(8,128)(2,1)} copy(bf16[256,1536]{1,0:T(8,128)(2,1)S(1)} %get-tuple-element.4) | data formatting | bytes 1572864

commit v5 on v4

--- a/solution.py
+++ b/solution.py
@@ -17,6 +17,7 @@
 R2 = BLK - R1
 S1 = ROWS // 2
 C1 = COLS // 2
+CODE = S1 + S1 // 3
 ZBLK = NX * BLK
 PIECE = 2 * NX * ROWS
 F32, BF16 = jnp.float32, jnp.bfloat16
@@ -24,7 +25,7 @@
 
 
 def kernel(attn, w, cot, proj, igrad, wgrad, A, AH, AO, CQ, PM, Wp, Wr, Wx, cotp, cotx, pv, iv, G, bo, bm, br,
-           xa, xb, za, za4, ya, yb, yxa, yxb, wv, send, recv, local):
+           xa, xb, za, za4, ya, yb, yxa, yxb, xe, xh, ze, ye, yxe, wv, send, recv, local):
     row, c, y = lax.axis_index("row"), lax.axis_index("col"), lax.axis_index("depth")
     z, x = row // NX, lax.rem(row, NX)
 
@@ -242,25 +243,68 @@
             G[4 * i + four(ka)] = g[0]
             G[4 * i + four(kb)] = g[1]
 
+    def chunks(ref, of):
+        wide = min(ref.shape[-1], 384)
+
+        @pl.loop(0, ref.shape[-1] // wide)
+        def _(i):
+            of(pl.ds(pl.multiple_of(i * wide, wide), wide))
+
+    def last_place(top):
+        top = jnp.abs(top)
+        return (top * (1.0 + 1.02 * 2.0**-8)).astype(BF16).astype(F32) - top
+
+    def encode(v):
+        top = v.astype(BF16).astype(F32)
+        unit = jnp.maximum(last_place(top), 1e-30)
+        q = jnp.clip(jnp.floor((v - top) * pl.reciprocal(unit, approx=True) * 5.0 + 0.5), -2.0, 2.0)
+        n = S1 // 3
+        low = q[0:n] * 25.0 + q[n:2 * n] * 5.0 + q[2 * n:]
+        return jnp.concatenate([top, low], axis=0).astype(BF16)
+
+    def decode(e):
+        e = e.astype(F32)
+        top, low = e[0:S1], e[S1:]
+        q0 = jnp.floor((low + 12.5) * (1.0 / 25.0))
+        low = low - 25.0 * q0
+        q1 = jnp.floor((low + 2.5) * (1.0 / 5.0))
+        q = jnp.concatenate([q0, q1, low - 5.0 * q1], axis=0)
+        return top + last_place(top) * (q * 0.2)
+
+    def collect(dst, *arrived):
+        def add(cols):
+            dst[:, cols] += sum(decode(a[:, cols]) for a in arrived)
+
+        chunks(dst, add)
+
     lo, hi = pl.ds(0, C1), pl.ds(C1, C1)
     ra, rb = pl.ds(0, S1), pl.ds(S1, S1)
 
+    def onward(g, arrived, out, there, dev):
+        def one(cols):
+            out[:, cols] = encode(g[:, cols] if arrived is None else g[:, cols] + decode(arrived[:, cols]))
+
+        chunks(out, one)
+        return push(out, there, dev)
+
     def sumx(k):
-        gx[k, 0] = push(G.at[zz(k), xx(2), ra, lo], xa.at[k % NZ, 0], xp)
-        gx[k, 1] = push(G.at[zz(k), xx(2), ra, hi], xa.at[k % NZ, 1], xm)
+        n = k % NZ
+        gx[k, 0] = onward(G.at[zz(k), xx(2), ra, lo], None, xh.at[n, 0], xa.at[n, 0], xp)
+        gx[k, 1] = onward(G.at[zz(k), xx(2), ra, hi], None, xh.at[n, 1], xa.at[n, 1], xm)
 
     def sumx_on(k):
+        n = k % NZ
         gx[k, 0].wait_recv()
-        G[zz(k), xx(1), 0:S1, 0:C1] += xa[k % NZ, 0]
-        gx[k, 2] = push(G.at[zz(k), xx(1), ra], xb.at[k % NZ, 0], xp)
+        collect(G.at[zz(k), xx(1), ra, lo], xa.at[n, 0])
+        gx[k, 2] = onward(G.at[zz(k), xx(1), ra], None, xe.at[n, 0], xb.at[n, 0], xp)
         gx[k, 1].wait_recv()
-        G[zz(k), xx(-1), 0:S1, C1:] += xa[k % NZ, 1]
-        gx[k, 3] = push(G.at[zz(k), xx(-1), ra], xb.at[k % NZ, 1], xm)
+        collect(G.at[zz(k), xx(-1), ra, hi], xa.at[n, 1])
+        gx[k, 3] = onward(G.at[zz(k), xx(-1), ra], None, xe.at[n, 1], xb.at[n, 1], xm)
 
     def sumx_in(k):
         gx[k, 2].wait_recv()
         gx[k, 3].wait_recv()
-        G[zz(k), x, 0:S1] += xb[k % NZ, 0] + xb[k % NZ, 1]
+        collect(G.at[zz(k), x, ra], xb.at[k % NZ, 0], xb.at[k % NZ, 1])
 
     def sumz(step):
         if step == 1:
@@ -269,37 +313,35 @@
             return
         gz[step - 1, 0].wait_recv()
         gz[step - 1, 1].wait_recv()
+        if step == 5:
+            collect(G.at[z, x, ra], za.at[2, 0], za.at[2, 1])
+            return
         if step == 2:
             G[zz(3), x, 0:S1, 0:C1] += za4[0]
             G[zz(-3), x, 0:S1, C1:] += za4[1]
-        elif step < 5:
-            G[zz(5 - step), x, 0:S1] += za[step - 3, 0]
-            G[zz(step - 5), x, 0:S1] += za[step - 3, 1]
-        else:
-            G[z, x, 0:S1] += za[2, 0] + za[2, 1]
-            return
-        gz[step, 0] = push(G.at[zz(5 - step), x, ra], za.at[step - 2, 0], zp)
-        gz[step, 1] = push(G.at[zz(step - 5), x, ra], za.at[step - 2, 1], zm)
+        for i, dev in ((0, zp), (1, zm)):
+            g = G.at[zz((5 - step) * (1 - 2 * i)), x, ra]
+            gz[step, i] = onward(g, None if step == 2 else za.at[step - 3, i], ze.at[step - 2, i], za.at[step - 2, i], dev)
 
     def sumy(step, j):
-        i, d = xx(j), j % NX
+        n, d = xx(j), j % NX
         if step == 1:
-            gy[1, j, 0] = push(G.at[zz(4), i, rb, lo], yb.at[0, d], zp)
-            gy[1, j, 1] = push(G.at[zz(4), i, rb, hi], yb.at[1, d], zm)
+            gy[1, j, 0] = push(G.at[zz(4), n, rb, lo], yb.at[0, d], zp)
+            gy[1, j, 1] = push(G.at[zz(4), n, rb, hi], yb.at[1, d], zm)
             return
         gy[step - 1, j, 0].wait_recv()
         gy[step - 1, j, 1].wait_recv()
+        if step == 5:
+            collect(G.at[z, n, rb], ya.at[2, 0, d], ya.at[2, 1, d])
+            return
         if step == 2:
-            G[zz(3), i, S1:, 0:C1] += yb[0, d]
-            G[zz(-3), i, S1:, C1:] += yb[1, d]
-        elif step < 5:
-            G[zz(5 - step), i, S1:] += ya[step - 3, 0, d]
-            G[zz(step - 5), i, S1:] += ya[step - 3, 1, d]
-        else:
-            G[z, i, S1:] += ya[2, 0, d] + ya[2, 1, d]
-            return
-        gy[step, j, 0] = push(G.at[zz(5 - step), i, rb], ya.at[step - 2, 0, d], zp)
-        gy[step, j, 1] = push(G.at[zz(step - 5), i, rb], ya.at[step - 2, 1, d], zm)
+            G[zz(3), n, S1:, 0:C1] += yb[0, d]
+            G[zz(-3), n, S1:, C1:] += yb[1, d]
+        for i, dev in ((0, zp), (1, zm)):
+            g = G.at[zz((5 - step) * (1 - 2 * i)), n, rb]
+            gy[step, j, i] = onward(
+                g, None if step == 2 else ya.at[step - 3, i, d], ye.at[step - 2, i, d], ya.at[step - 2, i, d], dev
+            )
 
     def sumyx():
         gyx[0] = push(G.at[z, xx(2), rb, lo], yxa.at[0], xp)
@@ -308,10 +350,10 @@
     def sumyx_on():
         gyx[0].wait_recv()
         G[z, xx(1), S1:, 0:C1] += yxa[0]
-        gyx[2] = push(G.at[z, xx(1), rb], yxb.at[0], xp)
+        gyx[2] = onward(G.at[z, xx(1), rb], None, yxe.at[0], yxb.at[0], xp)
         gyx[1].wait_recv()
         G[z, xx(-1), S1:, C1:] += yxa[1]
-        gyx[3] = push(G.at[z, xx(-1), rb], yxb.at[1], xm)
+        gyx[3] = onward(G.at[z, xx(-1), rb], None, yxe.at[1], yxb.at[1], xm)
 
     def wout(r0, g):
         wv[r0:r0 + S1, :] = g * (1.0 / math.sqrt(TOK * NZ * NX * NY))
@@ -327,7 +369,7 @@
     def wout_y():
         gyx[2].wait_recv()
         gyx[3].wait_recv()
-        wout(S1, G[z, x, S1:] + (yxb[0] + yxb[1]))
+        wout(S1, G[z, x, S1:] + (decode(yxb[0]) + decode(yxb[1])))
 
     def fwd(src, lane0, width, at_col):
         p = jnp.dot(A[...], src[:, :, :, pl.ds(lane0, width)].reshape(NZ * ZBLK, width), preferred_element_type=F32)
@@ -395,13 +437,13 @@
             copy.wait()
 
     cots()
+    own()
     w_in()
     rx()
     zpush(1)
     xpush(0)
+    own_push()
     rpush(1, 0)
-    own()
-    own_push()
     perm(1)
     perm(2)
     rx_on()
@@ -413,150 +455,150 @@
     xpush(-1)
     xpush(1)
     rx_in()
+    rstep(1, 0)
+    att(2)
+    xstep(0)
     rpush(1, 2)
-    xstep(0)
-    att(2)
+    xstep(-1)
     rstep(1, -1)
-    xstep(-1)
+    cots_on()
+    cross(1)
+    zstep(2)
+    att_on(1)
+    xpush(2)
+    xlast(0)
+    xpush(-2)
     rstep(1, 1)
-    cots_on()
-    zstep(2)
-    xstep(1)
-    att_on(1)
-    cross(1)
-    xpush(-2)
-    xlast(0)
-    rstep(1, 2)
     xlast(-1)
-    xpush(2)
     cross(2)
     att_on(2)
+    rstep(2, -1)
+    xstep(1)
+    rstep(1, 2)
+    xstep(2)
+    rstep(2, 0)
+    ypush(0)
+    cross2(1)
+    xstep(-2)
     rstep(2, 1)
+    ypush(-1)
+    cross_in(1)
     xlast(1)
-    rstep(1, 0)
     zstep(3)
-    ypush(-1)
-    xstep(-2)
     xpush(-3)
-    cross2(1)
-    rstep(2, 2)
-    ypush(0)
-    cross_in(1)
-    rstep(3, 1)
-    xstep(2)
-    rstep(2, -1)
+    cots_in()
     ypush(1)
-    cots_in()
     term(1)
+    cross2(2)
+    ystep(0)
+    sumy(1, 1)
     sumy(1, 2)
-    sumy(1, 1)
     sumx(4)
-    ystep(-1)
-    cross2(2)
     xpush(3)
     sumy(1, -1)
-    zstep(4)
+    sumy(1, 0)
+    xlast(2)
     xlast(-2)
-    rstep(3, 2)
-    rstep(4, 1)
-    ystep(0)
-    xpush(4)
-    rstep(2, 0)
+    rstep(2, 2)
     ypush(-2)
     cross_in(2)
-    xlast(2)
     term(2)
+    xstep(-3)
     ypush(2)
     sumy(2, 2)
-    xstep(-3)
+    sumx(2)
+    sumx(3)
+    sumx(-3)
+    rstep(3, 0)
+    ystep(1)
+    sumx(-2)
+    ystep(-2)
+    rstep(3, 1)
+    sumx_on(4)
+    zstep(4)
     sumy(2, 1)
-    ystep(1)
+    sumy(2, -1)
+    xpush(4)
+    ystep(-1)
     ylast(0)
+    xlast(-3)
+    ystep(2)
+    rstep(3, 2)
+    sumy(3, 2)
+    rstep(4, 0)
+    ylast(1)
+    sumy(2, 0)
+    sumx_on(-3)
+    rstep(4, 1)
+    rstep(3, -1)
+    ypush(-3)
+    sumx_on(3)
+    sumx_in(4)
+    sumz(1)
+    ylast(-2)
     ylast(-1)
+    xstep(3)
+    sumy(3, 1)
     rstep(4, 2)
-    xstep(3)
-    rstep(3, -1)
-    sumy(2, -1)
-    ystep(-2)
-    sumx_on(4)
-    rstep(3, 0)
+    sumy(3, -1)
+    sumx_on(2)
+    ylast(2)
+    wcross(2)
+    sumy(4, 2)
     xstep(4)
-    ystep(2)
-    sumy(3, 2)
-    xlast(-3)
-    ypush(-3)
+    sumx_in(-3)
+    ystep(-3)
+    rstep(4, -1)
+    sumy(3, 0)
+    sumx_in(3)
+    sumx(1)
+    sumz(2)
     sumx(-1)
-    sumy(3, 1)
-    ylast(-2)
-    rstep(4, -1)
-    ylast(1)
-    sumx(3)
+    sumx(0)
     xlast(3)
     ypush(3)
-    sumx(-2)
-    sumy(1, 0)
-    sumx(-3)
-    sumy(3, -1)
-    sumx_in(4)
-    ylast(2)
-    wcross(2)
-    rstep(4, 0)
-    sumx(1)
-    sumx(2)
-    sumz(1)
+    sumy(4, 1)
+    sumx_on(-2)
+    sumx_in(2)
+    sumy(4, -1)
+    ylast(-3)
+    wcross(1)
+    sumy(5, 2)
+    sumyx()
     xlast(4)
     ypush(4)
-    fwd_main()
-    sumy(4, 2)
-    sumx_on(3)
+    bwd_other()
+    sumx_on(-1)
+    sumy(4, 0)
     ystep(3)
-    sumy(4, 1)
-    sumx_on(-3)
-    sumy(2, 0)
-    sumx_on(-2)
-    ystep(-3)
+    sumx_on(1)
+    sumx_in(-2)
+    sumz(3)
+    sumy(5, 1)
+    sumy(5, -1)
+    sumyx_on()
+    sumx_on(0)
+    ystep(4)
     bwd_own()
-    sumx_on(2)
-    sumy(4, -1)
-    ystep(4)
-    bwd_other()
-    sumx_in(3)
-    sumy(5, 2)
-    sumyx()
-    sumx_in(-3)
-    sumz(2)
-    sumy(5, 1)
-    sumx(0)
-    sumx_on(1)
-    ylast(3)
-    wcross(3)
-    ylast(-3)
-    wcross(1)
-    sumx_in(-2)
-    sumy(3, 0)
-    ylast(4)
-    wcross(4)
-    fwd_rest()
-    sumx_on(-1)
-    sumy(5, -1)
-    sumx_in(2)
-    sumyx_on()
-    sumz(3)
-    bwd_in()
-    bwd_out(2)
-    sumx_on(0)
-    bwd_out(3)
-    sumy(4, 0)
+    sumx_in(-1)
     sumx_in(1)
-    bwd_out(1)
-    bwd_out(4)
-    sumx_in(-1)
     sumz(4)
     sumy(5, 0)
     wout_y()
+    fwd_main()
     sumx_in(0)
     sumz(5)
     wout_x()
+    ylast(4)
+    wcross(4)
+    ylast(3)
+    wcross(3)
+    fwd_rest()
+    bwd_in()
+    bwd_out(1)
+    bwd_out(2)
+    bwd_out(4)
+    bwd_out(3)
 
     for k in sorted(last):
         last[k].wait_recv()
@@ -567,25 +609,33 @@
 
 
 def pass_on(*refs):
+    copies = [pltpu.make_async_copy(refs[i], refs[i + 3], refs[6].at[i]) for i in range(3)]
     for i in range(3):
-        refs[i + 3][...] = refs[i][...]
+        copies[i].start()
+    for i in range(3):
+        copies[i].wait()
 
 
 def body(attn, w, cot):
     whole = pl.BlockSpec(memory_space=pl.ANY)
-    f32s = [
+    sums = [
         (NZ, NX, ROWS, COLS),
         (4, TOK, ZBLK),
         (4, TOK, ZBLK),
         (4, TOK, ZBLK),
-        (NZ, 2, S1, C1),
-        (NZ, 2, S1, COLS),
-        (3, 2, S1, COLS),
+        (NZ, 2, CODE, C1),
+        (NZ, 2, CODE, COLS),
+        (3, 2, CODE, COLS),
         (2, S1, C1),
-        (3, 2, NX, S1, COLS),
+        (3, 2, NX, CODE, COLS),
         (2, NX, S1, C1),
         (2, S1, C1),
-        (2, S1, COLS),
+        (2, CODE, COLS),
+        (NZ, 2, CODE, COLS),
+        (NZ, 2, CODE, C1),
+        (3, 2, CODE, COLS),
+        (3, 2, NX, CODE, COLS),
+        (2, CODE, COLS),
         (ROWS, COLS),
     ]
     rest = HALF - WIDE
@@ -600,14 +650,21 @@
         in_specs=[whole] * 3,
         out_specs=(whole,) * 3,
         scratch_shapes=[pltpu.VMEM(s, BF16) for s in bf16s]
-        + [pltpu.VMEM(s, F32) for s in f32s]
+        + [pltpu.VMEM(s, BF16 if s[-2] == CODE else F32) for s in sums]
         + [pltpu.SemaphoreType.DMA((N_MSG,)), pltpu.SemaphoreType.DMA((N_MSG,)), pltpu.SemaphoreType.DMA((20,))],
         compiler_params=pltpu.CompilerParams(
             collective_id=0, has_side_effects=True, vmem_limit_bytes=40 * 2**20
         ),
         name="projection",
     )(attn, w, cot)
-    return done
+    return pl.pallas_call(
+        pass_on,
+        out_shape=[jax.ShapeDtypeStruct(o.shape, o.dtype) for o in done],
+        in_specs=[whole] * 3,
+        out_specs=[whole] * 3,
+        scratch_shapes=[pltpu.SemaphoreType.DMA((3,))],
+        name="results",
+    )(*(pltpu.with_memory_space_constraint(o, pltpu.VMEM) for o in done))
 
 
 def solution(mesh):

time: 87.7 us -> 80.5 us (0.918)
  Pallas kernels: 83.7 us -> 79.6 us
  local copies, waits for them, and re-layouts: 2.58 us -> 0 us
    pallas_call x1, Pallas kernels: 83.7 us -> 78.2 us  [body(): pl.pallas_call(kernel, out_shape=outs, in_specs=[whole] * 3, out_specs=(w...]
    unnamed x3 -> x0, local copies, waits for them, and re-layouts: 2.58 us -> none
    pallas_call x0 -> x1, Pallas kernels: none -> 1.36 us  [body(): pl.pallas_call(pass_on, out_shape=[jax.ShapeDtypeStruct(o.shape, o.dtype)...]
where the time goes in v5:
time: 80.5 us; the launch traced here: 80.2 us
  Pallas kernels  79.6 us (99%)
    pallas_call x1, Pallas kernels, body(): pl.pallas_call(kernel, out_shape=outs, in_specs=[whole] * 3, out_specs=(w...  78.2 us

profile of v5, /device:TPU:16, one launch (start us, length us, event | category | flops | bytes accessed | tf_op | source)
XLA Modules:
  0.0 80.2 jit_solution(4621565511064659644)
XLA Ops:
  0.6 78.2 %projection.1 = (bf16[256,1536]{1,0:T(8,128)(2,1)S(1)}, bf16[256,1536]{1,0:T(8,128)(2,1)S(1)}, f32[96,1536]{1,0:T(8,128)S(1)}) custom-call(bf16[256,1536]{1,0:T(8,128)(2,1)} %attn.1, bf16[96,1536]{1,0:T(8,128)(2,1)} %w.1, bf16[256,1536]{1,0:T(8,128)(2,1)} %cot.1), custom_call_target="tpu_custom_call" | custom-call | tf_op jit(solution)/shard_map/projection/pallas_call | solution.py:647
  78.9 1.4 %results.1 = (bf16[256,1536]{1,0:T(8,128)(2,1)}, bf16[256,1536]{1,0:T(8,128)(2,1)}, f32[96,1536]{1,0:T(8,128)}) custom-call(bf16[256,1536]{1,0:T(8,128)(2,1)S(1)} %get-tuple-element.6.refs_0_, bf16[256,1536]{1,0:T(8,128)(2,1)S(1)} %get-tuple-element.7.refs_1_, f32[96,1536]{1,0:T(8,128)S(1)} %get-tuple-element.8.refs_2_), custom_call_target="tpu_custom_call" | custom-call | tf_op jit(solution)/shard_map/results/pallas_call | solution.py:660

commit v6 on v5

--- a/solution.py
+++ b/solution.py
@@ -579,7 +579,6 @@
     sumyx_on()
     sumx_on(0)
     ystep(4)
-    bwd_own()
     sumx_in(-1)
     sumx_in(1)
     sumz(4)
@@ -593,6 +592,7 @@
     wcross(4)
     ylast(3)
     wcross(3)
+    bwd_own()
     fwd_rest()
     bwd_in()
     bwd_out(1)

time: 80.5 us -> 81 us (level)
  no operation moved by 1% of the time
where the time goes in v6:
time: 81 us; the launch traced here: 80.4 us
  Pallas kernels  79.7 us (98%)
    pallas_call x1, Pallas kernels, body(): pl.pallas_call(kernel, out_shape=outs, in_specs=[whole] * 3, out_specs=(w...  78.4 us

profile of v6, /device:TPU:16, one launch (start us, length us, event | category | flops | bytes accessed | tf_op | source)
XLA Modules:
  0.0 80.4 jit_solution(8227872690172950220)
XLA Ops:
  0.6 78.4 %projection.1 = (bf16[256,1536]{1,0:T(8,128)(2,1)S(1)}, bf16[256,1536]{1,0:T(8,128)(2,1)S(1)}, f32[96,1536]{1,0:T(8,128)S(1)}) custom-call(bf16[256,1536]{1,0:T(8,128)(2,1)} %attn.1, bf16[96,1536]{1,0:T(8,128)(2,1)} %w.1, bf16[256,1536]{1,0:T(8,128)(2,1)} %cot.1), custom_call_target="tpu_custom_call" | custom-call | tf_op jit(solution)/shard_map/projection/pallas_call | solution.py:647
  79.0 1.4 %results.1 = (bf16[256,1536]{1,0:T(8,128)(2,1)}, bf16[256,1536]{1,0:T(8,128)(2,1)}, f32[96,1536]{1,0:T(8,128)}) custom-call(bf16[256,1536]{1,0:T(8,128)(2,1)S(1)} %get-tuple-element.6.refs_0_, bf16[256,1536]{1,0:T(8,128)(2,1)S(1)} %get-tuple-element.7.refs_1_, f32[96,1536]{1,0:T(8,128)S(1)} %get-tuple-element.8.refs_2_), custom_call_target="tpu_custom_call" | custom-call | tf_op jit(solution)/shard_map/results/pallas_call | solution.py:660
